TPU v7x, 256 devices: a whole 4x4x8 slice. The times are simulated.
256 devices in a mesh: lat: 8 (over y, x_lo), lon: 32 (over z, x_hi, core).
Axes of the slice: x: 4 (x_hi: 2, x_lo: 2; x = x_hi * 2 + x_lo), y: 4, z: 8, core: 2. Of those that a mesh axis runs over, the one named last changes fastest.
Arguments:
- fine_tokens: bfloat16 [2, 48, 768, 512], P(None, 'lat', 'lon'), may hold values from -6 to 6
- grad_out: bfloat16 [2, 48, 768, 512], P(None, 'lat', 'lon'), may hold values from -6 to 6
- window_class: int32 [2, 48, 768], P(None, 'lat', 'lon'), may hold values from 0 to 2
- temper_fine: float32 [8], replicated, may hold values from 4 to 20
- temper_coarse: float32 [16], replicated, may hold values from 4 to 20
- gain_fine: float32 [512], replicated, may hold values from 0.1 to 1.9
- fine_qkv: bfloat16 [512, 1536], P('lon'), may hold values from -0.25 to 0.25
- fine_out: bfloat16 [512, 512], P('lon'), may hold values from -0.25 to 0.25
- gain_merge: float32 [2048], replicated, may hold values from 0.1 to 1.9
- merge_weight: bfloat16 [2048, 1024], P('lon'), may hold values from -0.125 to 0.125
- gain_coarse: float32 [1024], replicated, may hold values from 0.1 to 1.9
- coarse_qkv: bfloat16 [1024, 3072], P('lon'), may hold values from -0.1875 to 0.1875
- coarse_out: bfloat16 [1024, 1024], P('lon'), may hold values from -0.1875 to 0.1875
- split_weight: bfloat16 [1024, 2048], P('lon'), may hold values from -0.1875 to 0.1875
Outputs:
- output: bfloat16 [2, 48, 768, 512], P(None, 'lat', 'lon')
- grad_in: bfloat16 [2, 48, 768, 512], P(None, 'lat', 'lon')
All inputs are finite; a program needn't handle non-finite values.
Results may differ from a plain program's by a relative error of at most 0.035.
Values may be sent and summed in bfloat16 or wider, within the bound.
A program may use at most 128 MiB of HBM per device.

v0:
```python
import jax
import jax.numpy as jnp
from jax import lax
from jax.sharding import PartitionSpec as P

WL = 2
WLAT = 6
WLON = 12


LN_EPS = 1e-05
UNIT_EPS = 1e-06


def from_behind(shard, axis, by):
    devices = lax.axis_size(axis)
    return lax.ppermute(shard, axis, [(i, (i + by) % devices) for i in range(devices)])


def swapped(value, axis, distance):
    mask = 2**distance
    pairs = [(source, source ^ mask) for source in range(lax.axis_size(axis))]
    return lax.ppermute(value, axis, pairs)


def layer_norm(values, scales):
    average = jnp.mean(values, axis=-1, keepdims=True)
    centred = values - average
    spread = jnp.mean(centred * centred, axis=-1, keepdims=True)
    return (centred * lax.rsqrt(spread + LN_EPS) * scales).astype(jnp.bfloat16)


def unit_rows(values):
    widened = values.astype(jnp.float32)
    total = jnp.sum(widened * widened, axis=-1, keepdims=True)
    return (widened * lax.rsqrt(total + UNIT_EPS)).astype(jnp.bfloat16)


def to_windows(layout, win_rows):
    lev_count, row_count, col_count = (layout.shape[0], layout.shape[1], layout.shape[2])
    trailing = tuple(layout.shape[3:])
    blocks = layout.reshape(
        (lev_count // WL, WL, row_count // win_rows, win_rows, col_count // WLON, WLON) + trailing
    )
    order_list = (0, 2, 4, 1, 3, 5) + tuple(range(6, 6 + len(trailing)))
    return blocks.transpose(order_list).reshape((-1, WL * win_rows * WLON) + trailing)


def from_windows(blocks, dims_out, win_rows):
    lev_count, row_count, col_count = (dims_out[0], dims_out[1], dims_out[2])
    trailing = tuple(dims_out[3:])
    layout = blocks.reshape(
        (lev_count // WL, row_count // win_rows, col_count // WLON, WL, win_rows, WLON) + trailing
    )
    order_list = (0, 3, 1, 4, 2, 5) + tuple(range(6, 6 + len(trailing)))
    return layout.transpose(order_list).reshape(tuple(dims_out))


def attend(queries, key_rows, value_rows, temper, allowed):
    scores = jnp.einsum("wnhe,wmhe->whnm", queries, key_rows, preferred_element_type=jnp.float32)
    scores = scores * temper[None, :, None, None]
    weights = jnp.exp(scores)
    if allowed is not None:
        weights = jnp.where(allowed[:, None], weights, 0.0)
    chances = (weights / jnp.sum(weights, axis=-1, keepdims=True)).astype(jnp.bfloat16)
    mixed = jnp.einsum("whnm,wmhe->wnhe", chances, value_rows, preferred_element_type=jnp.float32)
    return mixed.astype(jnp.bfloat16).reshape(mixed.shape[0], mixed.shape[1], -1)


def window_block(layout, labels, qkv_weight, out_weight, temper):
    blocks = to_windows(layout, WLAT)
    win_count, tok_count, feat_count = blocks.shape
    head_count = temper.shape[0]
    head_size = qkv_weight.shape[1] // (3 * head_count)
    qkv_act = jnp.dot(
        blocks.reshape(-1, feat_count), qkv_weight, preferred_element_type=jnp.float32
    ).astype(jnp.bfloat16)
    qkv_act = qkv_act.reshape(win_count, tok_count, 3, head_count, head_size)
    marks = to_windows(labels, WLAT)
    allowed = marks[:, :, None] == marks[:, None, :]
    mixed = attend(
        unit_rows(qkv_act[:, :, 0]), unit_rows(qkv_act[:, :, 1]), qkv_act[:, :, 2], temper, allowed
    )
    delta = jnp.dot(
        mixed.reshape(win_count * tok_count, -1), out_weight, preferred_element_type=jnp.float32
    )
    return from_windows(
        delta.reshape(win_count, tok_count, -1),
        tuple(layout.shape[:3]) + (out_weight.shape[1],),
        WLAT,
    )


def merge_tokens(layout):
    lev_count, row_count, col_count, feat_count = layout.shape
    pieces = layout.reshape(lev_count, row_count // 2, 2, col_count // 2, 2, feat_count)
    pieces = pieces.transpose(0, 1, 3, 4, 2, 5)
    return pieces.reshape(lev_count, row_count // 2, col_count // 2, 4 * feat_count)


def split_tokens(layout, feat_count):
    lev_count, row_count, col_count = (layout.shape[0], layout.shape[1], layout.shape[2])
    pieces = layout.reshape(lev_count, row_count, col_count, 2, 2, feat_count).transpose(
        0, 1, 4, 2, 3, 5
    )
    return pieces.reshape(lev_count, 2 * row_count, 2 * col_count, feat_count)


def merge_section(hidden, scales, weight_all):
    merged = merge_tokens(hidden)
    merged_norm = layer_norm(merged.astype(jnp.float32), scales)
    lead_dims = tuple(merged_norm.shape[:3])
    coarse = jnp.dot(
        merged_norm.reshape(-1, merged_norm.shape[3]),
        weight_all,
        preferred_element_type=jnp.float32,
    )
    return coarse.astype(jnp.bfloat16).reshape(lead_dims + (weight_all.shape[1],))


def split_section(coarse_next, weight_all):
    lead_dims = tuple(coarse_next.shape[:3])
    spread_out = jnp.dot(
        coarse_next.reshape(-1, coarse_next.shape[3]),
        weight_all,
        preferred_element_type=jnp.float32,
    )
    return split_tokens(
        spread_out.reshape(lead_dims + (weight_all.shape[1],)), weight_all.shape[1] // 4
    )


def fetch_ahead(layout):
    col_shift = WLON // 2
    row_shift = WLAT // 2
    across = from_behind(layout[:, :, :col_shift], "lon", -1)
    moved = jnp.concatenate([layout[:, :, col_shift:], across], axis=2)
    below = from_behind(moved[:, :row_shift], "lat", -1)
    return jnp.concatenate([moved[:, row_shift:], below], axis=1)


def send_behind(layout):
    col_shift = WLON // 2
    row_shift = WLAT // 2
    col_keep = layout.shape[2] - col_shift
    above = from_behind(layout[:, row_shift:], "lat", 1)
    moved = jnp.concatenate([above, layout[:, :row_shift]], axis=1)
    back_cols = from_behind(moved[:, :, col_keep:], "lon", 1)
    return jnp.concatenate([back_cols, moved[:, :, :col_keep]], axis=2)


def gather_quad(layout):
    partner = swapped(layout, "lat", 0)
    low_lat = lax.axis_index("lat") % 2 == 0
    paired = jnp.where(
        low_lat,
        jnp.concatenate([layout, partner], axis=1),
        jnp.concatenate([partner, layout], axis=1),
    )
    across = swapped(paired, "lon", 0)
    low_lon = lax.axis_index("lon") % 2 == 0
    return jnp.where(
        low_lon,
        jnp.concatenate([paired, across], axis=2),
        jnp.concatenate([across, paired], axis=2),
    )


def sum_quad(partial_all):
    half_cols = partial_all.shape[2] // 2
    col_half = lax.axis_index("lon") % 2
    keep_cols = lax.dynamic_slice_in_dim(partial_all, col_half * half_cols, half_cols, 2)
    send_cols = lax.dynamic_slice_in_dim(partial_all, (1 - col_half) * half_cols, half_cols, 2)
    paired = keep_cols + swapped(send_cols.astype(jnp.bfloat16), "lon", 0).astype(send_cols.dtype)
    half_rows = paired.shape[1] // 2
    row_half = lax.axis_index("lat") % 2
    keep_rows = lax.dynamic_slice_in_dim(paired, row_half * half_rows, half_rows, 1)
    send_rows = lax.dynamic_slice_in_dim(paired, (1 - row_half) * half_rows, half_rows, 1)
    return keep_rows + swapped(send_rows.astype(jnp.bfloat16), "lat", 0).astype(send_rows.dtype)


def heads_forward(coarse_norm, qkv_all, out_all, temper):
    quad_norm = gather_quad(coarse_norm)
    head_total = temper.shape[0]
    head_share = head_total // 4
    feat_count = qkv_all.shape[0]
    head_size = feat_count // head_total
    group_index = 2 * (lax.axis_index("lat") % 2) + lax.axis_index("lon") % 2
    qkv_cols = lax.dynamic_slice_in_dim(
        qkv_all.reshape(feat_count, 3, head_total, head_size),
        group_index * head_share,
        head_share,
        2,
    )
    qkv_cols = qkv_cols.reshape(feat_count, 3 * head_share * head_size)
    out_rows = lax.dynamic_slice_in_dim(
        out_all, group_index * head_share * head_size, head_share * head_size, 0
    )
    temper_share = lax.dynamic_slice_in_dim(temper, group_index * head_share, head_share, 0)
    blocks = to_windows(quad_norm, WLAT)
    win_count, tok_count = (blocks.shape[0], blocks.shape[1])
    qkv_act = jnp.dot(
        blocks.reshape(-1, feat_count), qkv_cols, preferred_element_type=jnp.float32
    ).astype(jnp.bfloat16)
    qkv_act = qkv_act.reshape(win_count, tok_count, 3, head_share, head_size)

    def core_mix(parts):
        return attend(
            unit_rows(parts[:, :, 0]), unit_rows(parts[:, :, 1]), parts[:, :, 2], temper_share, None
        )

    mixed, core_pull = jax.vjp(core_mix, qkv_act)
    partial_rows = jnp.dot(
        mixed.reshape(win_count * tok_count, -1), out_rows, preferred_element_type=jnp.float32
    )
    coarse_delta = sum_quad(
        from_windows(partial_rows.reshape(win_count, tok_count, feat_count), quad_norm.shape, WLAT)
    )

    def backward(grad_next):
        grad_quad = to_windows(gather_quad(grad_next), WLAT).reshape(-1, feat_count)
        grad_mixed = jnp.dot(grad_quad, out_rows.T, preferred_element_type=jnp.float32).astype(
            jnp.bfloat16
        )
        (grad_qkv,) = core_pull(grad_mixed.reshape(mixed.shape))
        grad_part = jnp.dot(
            grad_qkv.reshape(win_count * tok_count, -1),
            qkv_cols.T,
            preferred_element_type=jnp.float32,
        )
        grad_layout = from_windows(
            grad_part.reshape(win_count, tok_count, feat_count), quad_norm.shape, WLAT
        )
        return sum_quad(grad_layout).astype(jnp.bfloat16)

    return (coarse_delta, backward)


def per_device(
    fine_tokens,
    grad_out,
    window_class,
    temper_fine,
    temper_coarse,
    gain_fine,
    fine_qkv,
    fine_out,
    gain_merge,
    merge_weight,
    gain_coarse,
    coarse_qkv,
    coarse_out,
    split_weight,
):
    fine_qkv_all, fine_out_all, merge_all, coarse_qkv_all, coarse_out_all, split_all = (
        lax.all_gather(fine_qkv, "lon", axis=0, tiled=True),
        lax.all_gather(fine_out, "lon", axis=0, tiled=True),
        lax.all_gather(merge_weight, "lon", axis=0, tiled=True),
        lax.all_gather(coarse_qkv, "lon", axis=0, tiled=True),
        lax.all_gather(coarse_out, "lon", axis=0, tiled=True),
        lax.all_gather(split_weight, "lon", axis=0, tiled=True),
    )
    wide_in = fine_tokens.astype(jnp.float32)
    normed, norm_pull = jax.vjp(lambda values: layer_norm(values, gain_fine), wide_in)
    region = fetch_ahead(normed)
    row_index = jnp.arange(window_class.shape[1])
    at_pole = (lax.axis_index("lat") == lax.axis_size("lat") - 1) & (
        row_index >= window_class.shape[1] - WLAT // 2
    )
    labels = window_class + 3 * at_pole.astype(jnp.int32)[None, :, None]

    def fine_part(inputs):
        return window_block(inputs, labels, fine_qkv_all, fine_out_all, temper_fine).astype(
            jnp.bfloat16
        )

    region_out, fine_pull = jax.vjp(fine_part, region)
    fine_delta = send_behind(region_out)
    hidden = (wide_in + fine_delta.astype(jnp.float32)).astype(jnp.bfloat16)
    coarse, merge_pull = jax.vjp(
        lambda values: merge_section(values, gain_merge, merge_all), hidden
    )
    coarse_wide = coarse.astype(jnp.float32)
    coarse_norm, coarse_norm_pull = jax.vjp(
        lambda values: layer_norm(values, gain_coarse), coarse_wide
    )
    coarse_delta, coarse_back = heads_forward(
        coarse_norm, coarse_qkv_all, coarse_out_all, temper_coarse
    )
    coarse_next = (coarse_wide + coarse_delta).astype(jnp.bfloat16)
    split_add, split_pull = jax.vjp(lambda values: split_section(values, split_all), coarse_next)
    output = (hidden.astype(jnp.float32) + split_add).astype(jnp.bfloat16)
    (grad_next,) = split_pull(grad_out.astype(jnp.float32))
    grad_normed_coarse = coarse_back(grad_next)
    (grad_wide,) = coarse_norm_pull(grad_normed_coarse)
    grad_coarse = (grad_next.astype(jnp.float32) + grad_wide).astype(jnp.bfloat16)
    (grad_merge,) = merge_pull(grad_coarse)
    grad_hidden = grad_out + grad_merge
    grad_region = fetch_ahead(grad_hidden)
    (grad_region_in,) = fine_pull(grad_region)
    grad_normed = send_behind(grad_region_in)
    (grad_wide_in,) = norm_pull(grad_normed)
    grad_in = (grad_hidden.astype(jnp.float32) + grad_wide_in).astype(jnp.bfloat16)
    return (output, grad_in)


def solution(mesh):
    return jax.shard_map(
        per_device,
        mesh=mesh,
        in_specs=(
            P(None, "lat", "lon", None),
            P(None, "lat", "lon", None),
            P(None, "lat", "lon"),
            P(),
            P(),
            P(),
            P("lon", None),
            P("lon", None),
            P(),
            P("lon", None),
            P(),
            P("lon", None),
            P("lon", None),
            P("lon", None),
        ),
        out_specs=(P(None, "lat", "lon", None), P(None, "lat", "lon", None)),
        check_vma=False,
    )
```

profile of v0, /device:TPU:0, one launch (start us, length us, event | category | flops | bytes accessed | tf_op | source)
XLA Modules:
  0.0 574.1 jit_solution(17030957467710839171)
XLA Ops:
  14.7 6.1 %collective-permute-start = (bf16[2,6,6,512]{3,0,2,1:T(2,128)(2,1)S(1)}, bf16[2,6,6,512]{3,0,2,1:T(2,128)(2,1)S(1)}, u32[]{:S(2)}, u32[]{:S(2)}) collective-permute-start(bf16[2,6,6,512]{3,0,2,1:T(2,128)(2,1)S(1)} %slice.89), channel_id=1, source_target_pairs={{0,31},{1,0},{2,1},{3,2},{4,3},{5,4},{6,5},{7,6},{8,7},{9,8},{10,9... | collective-permute-start | bytes 221192 | tf_op jit(solution)/shard_map/ppermute | solution.py:17
  20.8 41.2 %all_gather.19 = bf16[512,512]{1,0:T(8,128)(2,1)} all-gather(bf16[16,512]{1,0:T(8,128)(2,1)S(1)} %copy-done.49), channel_id=1, replica_groups=mesh['lat'=8,'lon'=32] {'lon'}, dimensions={0}, use_global_device_ids=true | all-gather | bytes 540672 | tf_op jit(solution)/shard_map/all_gather | solution.py:257
  62.8 3.9 collective-permute-start.1
  66.8 3.5 collective-permute-done.1
  70.9 22.1 %all-gather.6.cloned.1.call-done = bf16[512,1536]{1,0:T(8,128)(2,1)} async-done(((bf16[16,1536]{1,0:T(8,128)(2,1)}), bf16[512,1536]{1,0:T(8,128)(2,1)}) %all-gather.6.cloned.1.call-update) | async-done | bytes 1572880 | tf_op jit(solution)/shard_map/all_gather | solution.py:256
  105.9 8.1 %collective-permute-done.2 = bf16[2,3,24,512]{3,0,2,1:T(2,128)(2,1)S(1)} collective-permute-done((bf16[2,3,24,512]{3,0,2,1:T(2,128)(2,1)S(1)}, bf16[2,3,24,512]{3,0,2,1:T(2,128)(2,1)S(1)}, u32[]{:S(2)}, u32[]{:S(2)}) %collective-permute-start.2) | collective-permute-done | bytes 147488 | tf_op jit(solution)/shard_map/ppermute | solution.py:17
  115.7 6.2 %collective-permute-done.3 = bf16[2,6,6,512]{3,0,2,1:T(2,128)(2,1)S(1)} collective-permute-done((bf16[2,6,6,512]{3,0,2,1:T(2,128)(2,1)S(1)}, bf16[2,6,6,512]{3,0,2,1:T(2,128)(2,1)S(1)}, u32[]{:S(2)}, u32[]{:S(2)}) %collective-permute-start.3) | collective-permute-done | bytes 73760 | tf_op jit(solution)/shard_map/ppermute | solution.py:17
  126.7 52.4 %all-gather.14.cloned.1.call-done = bf16[1024,2048]{1,0:T(8,128)(2,1)} async-done(((bf16[32,2048]{1,0:T(8,128)(2,1)}), bf16[1024,2048]{1,0:T(8,128)(2,1)}) %all-gather.14.cloned.1.call-update) | async-done | bytes 4194320 | tf_op jit(solution)/shard_map/all_gather | solution.py:261
  179.1 3.6 convolution_convert_fusion.17
  183.9 81.4 %all-gather.8.cloned.1.call-done = bf16[2048,1024]{1,0:T(8,128)(2,1)} async-done(((bf16[64,1024]{1,0:T(8,128)(2,1)}), bf16[2048,1024]{1,0:T(8,128)(2,1)}) %all-gather.8.cloned.1.call-update) | async-done | bytes 4194320 | tf_op jit(solution)/shard_map/all_gather | solution.py:258
  265.4 3.2 fusion.105
  273.8 6.4 %copy.112 = bf16[2048,1024]{1,0:T(8,128)(2,1)} copy(bf16[2048,1024]{0,1:T(8,128)(2,1)} %bitcast.208) | data formatting | bytes 8388608 | tf_op jit(solution)/shard_map/jvp()/dot_general | solution.py:123
  288.4 56.2 %all-gather.12.cloned.1.call-done = bf16[1024,1024]{1,0:T(8,128)(2,1)} async-done(((bf16[32,1024]{1,0:T(8,128)(2,1)}), bf16[1024,1024]{1,0:T(8,128)(2,1)}) %all-gather.12.cloned.1.call-update) | async-done | bytes 2097168 | tf_op jit(solution)/shard_map/all_gather | solution.py:260
  344.7 2.2 convolution_convert_fusion.16
  354.4 84.1 %all-gather.10.cloned.1.call-done = bf16[1024,3072]{1,0:T(8,128)(2,1)} async-done(((bf16[32,3072]{1,0:T(8,128)(2,1)}), bf16[1024,3072]{1,0:T(8,128)(2,1)}) %all-gather.10.cloned.1.call-update) | async-done | bytes 6291472 | tf_op jit(solution)/shard_map/all_gather | solution.py:259
  438.5 8.7 %copy.102 = bf16[1024,3072]{0,1:T(8,128)(2,1)} copy(bf16[1024,3072]{1,0:T(8,128)(2,1)} %all-gather.10.cloned.1.call-done) | data formatting | bytes 12582912 | tf_op jit(solution)/shard_map/all_gather | solution.py:259
  451.4 2.6 reshape.379
  454.0 2.3 fusion.102
  468.1 2.3 copy.155
  470.4 2.6 reshape.412
  473.1 2.4 convolution_bitcast_fusion.1
  494.7 4.5 fusion.6
  499.2 2.4 reshape.402
  511.8 3.1 collective-permute-start.13
  524.0 2.2 reshape.392
  526.2 2.3 copy.131
  530.2 2.8 fusion.5
  537.5 3.9 copy.136
  541.4 2.8 reshape.393
  548.2 3.7 convolution_bitcast_fusion.2
  552.4 3.3 collective-permute-done.14
  557.2 6.3 %collective-permute-done.15 = bf16[2,6,6,512]{3,0,2,1:T(2,128)(2,1)S(1)} collective-permute-done((bf16[2,6,6,512]{3,0,2,1:T(2,128)(2,1)S(1)}, bf16[2,6,6,512]{3,0,2,1:T(2,128)(2,1)S(1)}, u32[]{:S(2)}, u32[]{:S(2)}) %collective-permute-start.15) | collective-permute-done | bytes 73760 | tf_op jit(solution)/shard_map/ppermute | solution.py:17
  (313 shorter events, 119.8 us)
Async XLA Ops:
  7.2 13.6 %copy-start.49 = (bf16[16,512]{1,0:T(8,128)(2,1)S(1)}, bf16[16,512]{1,0:T(8,128)(2,1)}, u32[]{:S(2)}) copy-start(bf16[16,512]{1,0:T(8,128)(2,1)} %param.21) | copy-start | bytes 49156
  7.2 54.8 %copy-start.51 = (s32[2,6,24]{2,0,1:T(2,128)S(1)}, s32[2,6,24]{2,0,1:T(2,128)}, u32[]{:S(2)}) copy-start(s32[2,6,24]{2,0,1:T(2,128)} %param.16) | copy-start | bytes 3460
  7.2 85.8 %all-gather.6.cloned.1.call-start = ((), (), s32[]{:S(2)}) async-start(), calls=%async_computation | async-start | bytes 1622016 | tf_op jit(solution)/shard_map/all_gather | solution.py:256
  7.9 171.1 %all-gather.14.cloned.1.call-start = ((), (), s32[]{:S(2)}) async-start(), calls=%async_computation.4 | async-start | bytes 4325376 | tf_op jit(solution)/shard_map/all_gather | solution.py:261
  8.7 256.7 %all-gather.8.cloned.1.call-start = ((), (), s32[]{:S(2)}) async-start(), calls=%async_computation.1 | async-start | bytes 4325376 | tf_op jit(solution)/shard_map/all_gather | solution.py:258
  9.4 335.2 %all-gather.12.cloned.1.call-start = ((), (), s32[]{:S(2)}) async-start(), calls=%async_computation.3 | async-start | bytes 2162688 | tf_op jit(solution)/shard_map/all_gather | solution.py:260
  10.0 428.5 %all-gather.10.cloned.1.call-start = ((), (), s32[]{:S(2)}) async-start(), calls=%async_computation.2 | async-start | bytes 6488064 | tf_op jit(solution)/shard_map/all_gather | solution.py:259
  14.7 47.7 %collective-permute-start = (bf16[2,6,6,512]{3,0,2,1:T(2,128)(2,1)S(1)}, bf16[2,6,6,512]{3,0,2,1:T(2,128)(2,1)S(1)}, u32[]{:S(2)}, u32[]{:S(2)}) collective-permute-start(bf16[2,6,6,512]{3,0,2,1:T(2,128)(2,1)S(1)} %slice.89), channel_id=1, source_target_pairs={{0,31},{1,0},{2,1},{3,2},{4,3},{5,4},{6,5},{7,6},{8,7},{9,8},{10,9... | collective-permute-start | bytes 221192 | tf_op jit(solution)/shard_map/ppermute | solution.py:17
  62.8 7.6 %collective-permute-start.1 = (bf16[2,3,24,512]{3,0,2,1:T(2,128)(2,1)S(1)}, bf16[2,3,24,512]{3,0,2,1:T(2,128)(2,1)S(1)}, u32[]{:S(2)}, u32[]{:S(2)}) collective-permute-start(bf16[2,3,24,512]{3,0,2,1:T(2,128)(2,1)S(1)} %get-tuple-element.23), channel_id=1, source_target_pairs={{0,224},{32,0},{64,32},{96,64},{128,96},{160,128},{192,160},{224,1... | collective-permute-start | bytes 442376 | tf_op jit(solution)/shard_map/ppermute | solution.py:17
  66.8 34.3 %copy-start.31 = (pred[2,144,144]{1,2,0:T(8,128)(4,1)}, pred[2,144,144]{1,2,0:T(8,128)(4,1)S(1)}, u32[]{:S(2)}) copy-start(pred[2,144,144]{1,2,0:T(8,128)(4,1)S(1)} %broadcast_compare_fusion) | copy-start | bytes 124420
  103.9 10.6 %copy-start.33 = (f32[2048]{0:T(1024)S(1)}, f32[2048]{0:T(1024)}, u32[]{:S(2)}) copy-start(f32[2048]{0:T(1024)} %param.22) | copy-start | bytes 24580
  103.9 10.6 %copy-start.22 = (bf16[2,6,24,512]{3,2,1,0:T(8,128)(2,1)S(1)}, bf16[2,6,24,512]{3,2,1,0:T(8,128)(2,1)}, u32[]{:S(2)}) copy-start(bf16[2,6,24,512]{3,2,1,0:T(8,128)(2,1)} %param.15) | copy-start | bytes 884740
  104.5 10.6 %copy-start.61 = (f32[16]{0:T(128)S(1)}, f32[16]{0:T(128)}, u32[]{:S(2)}) copy-start(f32[16]{0:T(128)} %param.18) | copy-start | bytes 196
  104.8 9.2 %collective-permute-start.2 = (bf16[2,3,24,512]{3,0,2,1:T(2,128)(2,1)S(1)}, bf16[2,3,24,512]{3,0,2,1:T(2,128)(2,1)S(1)}, u32[]{:S(2)}, u32[]{:S(2)}) collective-permute-start(bf16[2,3,24,512]{3,0,2,1:T(2,128)(2,1)S(1)} %get-tuple-element.20), channel_id=1, source_target_pairs={{0,32},{32,64},{64,96},{96,128},{128,160},{160,192},{192,224},{224... | collective-permute-start | bytes 442376 | tf_op jit(solution)/shard_map/ppermute | solution.py:17
  114.1 7.8 %collective-permute-start.3 = (bf16[2,6,6,512]{3,0,2,1:T(2,128)(2,1)S(1)}, bf16[2,6,6,512]{3,0,2,1:T(2,128)(2,1)S(1)}, u32[]{:S(2)}, u32[]{:S(2)}) collective-permute-start(bf16[2,6,6,512]{3,0,2,1:T(2,128)(2,1)S(1)} %pad_maximum_fusion.7), channel_id=1, source_target_pairs={{0,1},{1,2},{2,3},{3,4},{4,5},{5,6},{6,7},{7,8},{8,9},{9,10},{10,1... | collective-permute-start | bytes 221192 | tf_op jit(solution)/shard_map/ppermute | solution.py:17
  124.3 141.1 %copy-start.52 = (f32[72]{0:T(128)}, f32[72]{0:T(128)S(1)}, u32[]{:S(2)}) copy-start(f32[72]{0:T(128)S(1)} %div.138) | copy-start | bytes 868
  125.0 57.7 %copy-start.41 = (f32[2,3,12]{2,1,0:T(4,128)}, f32[2,3,12]{2,1,0:T(4,128)S(1)}, u32[]{:S(2)}) copy-start(f32[2,3,12]{2,1,0:T(4,128)S(1)} %multiply_reduce_fusion.1) | copy-start | bytes 868
  125.1 140.3 %copy-start.54 = (f32[72]{0:T(128)}, f32[72]{0:T(128)S(1)}, u32[]{:S(2)}) copy-start(f32[72]{0:T(128)S(1)} %rsqrt.77) | copy-start | bytes 868
  183.4 86.2 %copy-start.34 = (f32[1024]{0:T(1024)S(1)}, f32[1024]{0:T(1024)}, u32[]{:S(2)}) copy-start(f32[1024]{0:T(1024)} %param.24) | copy-start | bytes 12292
  183.4 87.0 %collective-permute-start.8 = (bf16[2,3,12,1024]{3,2,1,0:T(8,128)(2,1)}, bf16[2,3,12,1024]{3,2,1,0:T(8,128)(2,1)}, u32[]{:S(2)}, u32[]{:S(2)}) collective-permute-start(bf16[2,3,12,1024]{3,2,1,0:T(8,128)(2,1)} %reshape.385), channel_id=1, source_target_pairs={{0,32},{32,0},{64,96},{96,64},{128,160},{160,128},{192,224},{224,1... | collective-permute-start | bytes 442376 | tf_op jit(solution)/shard_map/ppermute | solution.py:23
  269.7 10.5 %collective-permute-start.4 = (bf16[2,3,12,1024]{3,2,1,0:T(8,128)(2,1)S(1)}, bf16[2,3,12,1024]{3,2,1,0:T(8,128)(2,1)}, u32[]{:S(2)}, u32[]{:S(2)}) collective-permute-start(bf16[2,3,12,1024]{3,2,1,0:T(8,128)(2,1)S(1)} %multiply_convert_fusion.1), channel_id=1, source_target_pairs={{0,32},{32,0},{64,96},{96,64},{128,160},{160,128},{192,224},{224,1... | collective-permute-start | bytes 442376 | tf_op jit(solution)/shard_map/ppermute | solution.py:23
  272.5 10.5 %collective-permute-start.9 = (bf16[2,6,12,1024]{3,2,1,0:T(8,128)(2,1)}, bf16[2,6,12,1024]{3,2,1,0:T(8,128)(2,1)}, u32[]{:S(2)}, u32[]{:S(2)}) collective-permute-start(bf16[2,6,12,1024]{3,2,1,0:T(8,128)(2,1)} %maximum_select_fusion.3), channel_id=1, source_target_pairs={{0,1},{1,0},{2,3},{3,2},{4,5},{5,4},{6,7},{7,6},{8,9},{9,8},{10,11... | collective-permute-start | bytes 884744 | tf_op jit(solution)/shard_map/ppermute | solution.py:23
  282.1 66.8 %collective-permute-start.5 = (bf16[2,6,12,1024]{3,2,1,0:T(8,128)(2,1)}, bf16[2,6,12,1024]{3,2,1,0:T(8,128)(2,1)}, u32[]{:S(2)}, u32[]{:S(2)}) collective-permute-start(bf16[2,6,12,1024]{3,2,1,0:T(8,128)(2,1)} %maximum_select_fusion.2), channel_id=1, source_target_pairs={{0,1},{1,0},{2,3},{3,2},{4,5},{5,4},{6,7},{7,6},{8,9},{9,8},{10,11... | collective-permute-start | bytes 884744 | tf_op jit(solution)/shard_map/ppermute | solution.py:23
  478.5 4.6 collective-permute-start.10
  484.4 7.1 %collective-permute-start.11 = (bf16[2,3,12,1024]{3,2,1,0:T(8,128)(2,1)S(1)}, bf16[2,3,12,1024]{3,2,1,0:T(8,128)(2,1)S(1)}, u32[]{:S(2)}, u32[]{:S(2)}) collective-permute-start(bf16[2,3,12,1024]{3,2,1,0:T(8,128)(2,1)S(1)} %dynamic-slice_convert_fusion), channel_id=1, source_target_pairs={{0,32},{32,0},{64,96},{96,64},{128,160},{160,128},{192,224},{224,1... | collective-permute-start | bytes 442376 | tf_op jit(solution)/shard_map/ppermute | solution.py:23
  489.4 25.5 %collective-permute-start.6 = (bf16[2,6,12,1024]{3,2,1,0:T(8,128)(2,1)}, bf16[2,6,12,1024]{3,2,1,0:T(8,128)(2,1)}, u32[]{:S(2)}, u32[]{:S(2)}) collective-permute-start(bf16[2,6,12,1024]{3,2,1,0:T(8,128)(2,1)} %copy.193), channel_id=1, source_target_pairs={{0,1},{1,0},{2,3},{3,2},{4,5},{5,4},{6,7},{7,6},{8,9},{9,8},{10,11... | collective-permute-start | bytes 884744 | tf_op jit(solution)/shard_map/ppermute | solution.py:23
  508.0 3.5 collective-permute-start.12
  511.8 7.2 %collective-permute-start.13 = (bf16[2,3,24,512]{3,0,2,1:T(2,128)(2,1)S(1)}, bf16[2,3,24,512]{3,0,2,1:T(2,128)(2,1)S(1)}, u32[]{:S(2)}, u32[]{:S(2)}) collective-permute-start(bf16[2,3,24,512]{3,0,2,1:T(2,128)(2,1)S(1)} %get-tuple-element.19), channel_id=1, source_target_pairs={{0,224},{32,0},{64,32},{96,64},{128,96},{160,128},{192,160},{224,1... | collective-permute-start | bytes 442376 | tf_op jit(solution)/shard_map/ppermute | solution.py:17
  517.7 30.5 %collective-permute-start.7 = (bf16[2,3,12,1024]{3,2,1,0:T(8,128)(2,1)}, bf16[2,3,12,1024]{3,2,1,0:T(8,128)(2,1)}, u32[]{:S(2)}, u32[]{:S(2)}) collective-permute-start(bf16[2,3,12,1024]{3,2,1,0:T(8,128)(2,1)} %dynamic-slice_convert_fusion.1), channel_id=1, source_target_pairs={{0,32},{32,0},{64,96},{96,64},{128,160},{160,128},{192,224},{224,1... | collective-permute-start | bytes 442376 | tf_op jit(solution)/shard_map/ppermute | solution.py:23
  546.9 8.8 %collective-permute-start.14 = (bf16[2,3,24,512]{3,0,2,1:T(2,128)(2,1)S(1)}, bf16[2,3,24,512]{3,0,2,1:T(2,128)(2,1)S(1)}, u32[]{:S(2)}, u32[]{:S(2)}) collective-permute-start(bf16[2,3,24,512]{3,0,2,1:T(2,128)(2,1)S(1)} %get-tuple-element.16), channel_id=1, source_target_pairs={{0,32},{32,64},{64,96},{96,128},{128,160},{160,192},{192,224},{224... | collective-permute-start | bytes 442376 | tf_op jit(solution)/shard_map/ppermute | solution.py:17
  552.0 11.6 %copy-start.48 = (f32[512]{0:T(512)S(1)}, f32[512]{0:T(512)}, u32[]{:S(2)}) copy-start(f32[512]{0:T(512)} %param.19) | copy-start | bytes 6148
  555.8 7.7 %collective-permute-start.15 = (bf16[2,6,6,512]{3,0,2,1:T(2,128)(2,1)S(1)}, bf16[2,6,6,512]{3,0,2,1:T(2,128)(2,1)S(1)}, u32[]{:S(2)}, u32[]{:S(2)}) collective-permute-start(bf16[2,6,6,512]{3,0,2,1:T(2,128)(2,1)S(1)} %pad_maximum_fusion.6), channel_id=1, source_target_pairs={{0,1},{1,2},{2,3},{3,4},{4,5},{5,6},{6,7},{7,8},{8,9},{9,10},{10,1... | collective-permute-start | bytes 221192 | tf_op jit(solution)/shard_map/ppermute | solution.py:17
  (51 other events, 136.2 us)
Sparse Core Ops, SparseCore 0:
  10.8 82.1 all-gather.5
  95.8 83.2 all-gather.13
  181.8 83.4 all-gather.7
  268.0 76.6 all-gather.11
  347.3 91.1 all-gather.9
where the time goes:
time: 585 us; the launch traced here: 574 us
  waiting for transfers between devices  332 us (57%)
  local copies, waits for them, and re-layouts  88.5 us (15%)
  blocking collectives  41.2 us (7%)
  matrix products  40.7 us (7%)
  other arithmetic  35.2 us (6%)
  starting transfers between devices  21.2 us (4%)
  between operations  15.6 us (3%)
    all_gather x1, waiting for transfers between devices, per_device(): lax.all_gather(coarse_qkv, 'lon', axis=0, tiled=True)  84.1 us
    all_gather x1, waiting for transfers between devices, per_device(): lax.all_gather(merge_weight, 'lon', axis=0, tiled=True)  81.4 us
    all_gather x1, waiting for transfers between devices, per_device(): lax.all_gather(coarse_out, 'lon', axis=0, tiled=True)  56.2 us
    all_gather x1, waiting for transfers between devices, per_device(): lax.all_gather(split_weight, 'lon', axis=0, tiled=True)  52.4 us
    all_gather x1, blocking collectives, per_device(): lax.all_gather(fine_out, 'lon', axis=0, tiled=True)  41.2 us
    ppermute x8, waiting for transfers between devices, from_behind(): lax.ppermute(shard, axis, [(i, (i + by) % devices) for i in range(devices)])  30.3 us
    all_gather x1, waiting for transfers between devices, per_device(): lax.all_gather(fine_qkv, 'lon', axis=0, tiled=True)  22.1 us
    unnamed x134, local copies, waits for them, and re-layouts  18.3 us
  transfers between devices with their start and end apart: 21, of which 13 were waited for; matrix products, arithmetic and copies ran while one was open for 20% of the time, Pallas kernels for 0%

commit v1 on v0

v1 whole, which is shorter than its diff:
```python
import functools

import jax
import jax.numpy as jnp
import numpy as np
from jax import lax
from jax.experimental import pallas as pl
from jax.experimental.pallas import tpu as pltpu
from jax.sharding import PartitionSpec as P

MESH = pl.DeviceIdType.MESH
F32, BF16 = jnp.float32, jnp.bfloat16
LN_EPS = 1e-05
UNIT_EPS = 1e-06

LEV, ROWS, COLS = 2, 6, 24
NTOK = LEV * ROWS * COLS
NWIN = 144
NMINE = 72
HALO = 208
NCAT = 512
PIECES = ((0, 112), (112, 48), (160, 48))
PAD = 80


def layout_tables():
    flat = np.arange(NTOK).reshape(LEV, ROWS, COLS)
    merged_of = np.zeros(NTOK, np.int64)
    order = np.concatenate([flat[:, di::2, dj::2].reshape(-1) for dj in (0, 1) for di in (0, 1)])
    merged_of[order] = np.arange(NTOK)
    to_merged = np.zeros((NTOK, NTOK), np.float32)
    to_merged[np.arange(NTOK), order] = 1
    halo_slot = {}
    at = {"lat": 0, "lon": 112, "diag": 160}
    send = np.zeros((HALO, NTOK), np.float32)
    for l in range(LEV):
        for i in range(ROWS):
            for j in range(COLS):
                kind = {(1, 0): "lat", (0, 1): "lon", (1, 1): "diag"}.get((int(i < 3), int(j < 6)))
                if kind:
                    halo_slot[l, i, j] = at[kind]
                    send[at[kind], merged_of[flat[l, i, j]]] = 1
                    at[kind] += 1
    region = np.zeros((NTOK, NCAT), np.float32)
    row = 0
    for w in range(2):
        for l in range(LEV):
            for i in range(ROWS):
                for j in range(12):
                    si, sj = i + 3, 12 * w + j + 6
                    if si < ROWS and sj < COLS:
                        region[row, merged_of[flat[l, si, sj]]] = 1
                    else:
                        region[row, NTOK + halo_slot[l, si % ROWS, sj % COLS]] = 1
                    row += 1
    own, halo = region[:, :NTOK], region[:, NTOK:NTOK + HALO]
    back = np.zeros((NTOK, NCAT), np.float32)
    back[:, :NTOK] = own.T
    back[:, NTOK:NTOK + HALO] = send.T
    tables = (to_merged, to_merged.T, send, region, back, halo.T)
    return [np.ascontiguousarray(t).astype(jnp.bfloat16) for t in tables]


def dot(a, b, dims=((1,), (0,))):
    return lax.dot_general(a, b, (dims, ((), ())), preferred_element_type=F32)


TRANS_B = ((1,), (1,))
TRANS_A = ((0,), (0,))


def normalise(values):
    average = jnp.mean(values, axis=-1, keepdims=True)
    centred = values - average
    scale = lax.rsqrt(jnp.mean(centred * centred, axis=-1, keepdims=True) + LN_EPS)
    return centred * scale, scale


def norm_back(grad, gains, unit, scale):
    grad = grad * gains
    part = jnp.mean(grad, axis=-1, keepdims=True)
    along = jnp.mean(grad * unit, axis=-1, keepdims=True)
    return scale * (grad - part - unit * along)


def half_mask(rows):
    return lax.broadcasted_iota(jnp.int32, (rows, 128), 1) < 64


def half_sums(values, low):
    first = jnp.sum(jnp.where(low, values, 0.0), axis=-1, keepdims=True)
    second = jnp.sum(jnp.where(low, 0.0, values), axis=-1, keepdims=True)
    return jnp.where(low, first, second)


def attend_forward(act, mixed, chances, rows, first, temper, temper_at, allowed):
    low = half_mask(NWIN)

    def pair(p, carry):
        q = act[rows, pl.ds(pl.multiple_of(p * 128, 128), 128)].astype(F32)
        k = act[rows, pl.ds(pl.multiple_of(p * 128 + 512, 128), 128)].astype(F32)
        v = act[rows, pl.ds(pl.multiple_of(p * 128 + 1024, 128), 128)]
        q = q * lax.rsqrt(half_sums(q * q, low) + UNIT_EPS)
        k = (k * lax.rsqrt(half_sums(k * k, low) + UNIT_EPS)).astype(BF16)
        mixes = []
        for j in range(2):
            mine = low if j == 0 else jnp.logical_not(low)
            scores = dot(jnp.where(mine, q, 0.0).astype(BF16), k, TRANS_B) * temper[temper_at + 2 * p + j]
            weights = jnp.exp(scores)
            if allowed is not None:
                weights = weights * allowed
            chance = weights * (1.0 / jnp.sum(weights, axis=-1, keepdims=True))
            chances[first + 2 * p + j] = chance
            mixes.append(dot(chance.astype(BF16), v))
        mixed[rows, pl.ds(pl.multiple_of(p * 128, 128), 128)] = jnp.where(low, mixes[0], mixes[1]).astype(BF16)
        return carry

    lax.fori_loop(0, 4, pair, 0)


def attend_backward(act, grad_mixed, grad_act, chances, rows, first, temper, temper_at):
    low = half_mask(NWIN)

    def pair(p, carry):
        at = [pl.ds(pl.multiple_of(p * 128 + 512 * t, 128), 128) for t in range(3)]
        q, k, v = (act[rows, s].astype(F32) for s in at)
        q_scale = lax.rsqrt(half_sums(q * q, low) + UNIT_EPS)
        k_scale = lax.rsqrt(half_sums(k * k, low) + UNIT_EPS)
        q, k = q * q_scale, k * k_scale
        q_low, k_low = q.astype(BF16), k.astype(BF16)
        grad = grad_mixed[rows, at[0]]
        gq, gk, gv = [], [], []
        for j in range(2):
            mine = low if j == 0 else jnp.logical_not(low)
            chance = chances[first + 2 * p + j]
            gc = dot(grad, jnp.where(mine, v, 0.0).astype(BF16), TRANS_B)
            gc = chance * (gc - jnp.sum(gc * chance, axis=-1, keepdims=True))
            gs = (gc * temper[temper_at + 2 * p + j]).astype(BF16)
            gq.append(dot(gs, k_low))
            gk.append(dot(gs, q_low, TRANS_A))
            gv.append(dot(chance.astype(BF16), grad, TRANS_A))
        gq, gk, gv = (jnp.where(low, *parts) for parts in (gq, gk, gv))
        grad_act[rows, at[0]] = (q_scale * (gq - q * half_sums(gq * q, low))).astype(BF16)
        grad_act[rows, at[1]] = (k_scale * (gk - k * half_sums(gk * k, low))).astype(BF16)
        grad_act[rows, at[2]] = gv.astype(BF16)
        return carry

    lax.fori_loop(0, 4, pair, 0)


WEIGHTS = (
    ("fq", 16, 1536, True),
    ("fo", 16, 512, False),
    ("mw", 64, 1024, True),
    ("cq", 32, 1536, False),
    ("co", 32, 1024, False),
    ("sp", 32, 2048, True),
)
SEMS_PER_WEIGHT = 30


def kernel(
    x_ref, g_ref, marks_ref, temper_fine, temper_coarse, gain_fine, gain_merge, gain_coarse,
    fq_in, fo_in, mw_in, cq_in, co_in, sp_in,
    to_merged, from_merged, send_table, region_table, back_table, halo_table,
    out_ref, gin_ref,
    fq, fo, mw, cq, co, sp,
    buf0, buf1, buf2, buf3, sbuf0, sbuf1, sbuf2, sbuf3,
    prx, pry, prz, prw, psx, psy, psz, psw,
    xm_ref, act, mixed, gact, chances, hid, cact, cmixed, cchances, coarse_ref, cnext_ref, gnext_ref, mn_ref, wide_ref, gh_ref,
    sems, halo_sems, pair_sems,
):
    lat, lon = lax.axis_index("lat"), lax.axis_index("lon")
    y, x_lo = lat // 2, lat % 2
    z, x_hi, core = lon // 4, (lon // 2) % 2, lon % 2

    def at_lat(by):
        return lax.rem(lat + 8 + by, 8)

    def at_lon(by):
        return lax.rem(lon + 32 + by, 32)

    z_next, z_prev = (lat, at_lon(4)), (lat, at_lon(-4))
    y_next, y_prev = (at_lat(2), lon), (at_lat(-2), lon)
    x_mate = (lat + 1 - 2 * x_lo, lon + 2 - 4 * x_hi)
    sibling = (lat, lon + 1 - 2 * core)
    pair_mate = (lat + 1 - 2 * x_lo, lon)
    behind = ((at_lat(-1), lon), (lat, at_lon(-1)), (at_lat(-1), at_lon(-1)))
    ahead = ((at_lat(1), lon), (lat, at_lon(1)), (at_lat(1), at_lon(1)))
    friends = (z_next, z_prev, y_next, y_prev, x_mate) + behind + ahead

    unfinished = []

    def send(src, dst, sem_out, sem_in, device):
        copy = pltpu.make_async_remote_copy(
            src_ref=src, dst_ref=dst, send_sem=sem_out, recv_sem=sem_in, device_id=device, device_id_type=MESH
        )
        copy.start()
        return copy

    def arrived(dst, sem_out, sem_in, device):
        pltpu.make_async_remote_copy(
            src_ref=dst, dst_ref=dst, send_sem=sem_out, recv_sem=sem_in, device_id=device, device_id_type=MESH
        ).wait_recv()

    inputs = {"fq": fq_in, "fo": fo_in, "mw": mw_in, "cq": cq_in, "co": co_in, "sp": sp_in}
    buffers = {"fq": fq, "fo": fo, "mw": mw, "cq": cq, "co": co, "sp": sp}

    def weight_events(index):
        name, rows, cols, last_y = WEIGHTS[index]
        src, whole = inputs[name], buffers[name]
        width = cols // 4 if last_y else cols
        if last_y:
            columns = pl.ds(pl.multiple_of(y * width, 128), width)
        else:
            columns = slice(None)
        sem = [sems.at[index, i] for i in range(SEMS_PER_WEIGHT)]

        def block(zz):
            return whole.at[zz, :, core, :, columns]

        def stage_local():
            if name == "cq":
                for t in range(3):
                    from_at = pl.ds(pl.multiple_of(t * 1024 + x_lo * 512, 128), 512)
                    pltpu.make_async_copy(
                        src.at[:, from_at], whole.at[z, x_hi, core, :, pl.ds(t * 512, 512)], sem[t]
                    ).start()
            else:
                pltpu.make_async_copy(src.at[:, columns], whole.at[z, x_hi, core, :, columns], sem[0]).start()

        def stage_swap():
            if name == "cq":
                for t in range(3):
                    from_at = pl.ds(pl.multiple_of(t * 1024 + (1 - x_lo) * 512, 128), 512)
                    unfinished.append(send(
                        src.at[:, from_at], whole.at[z, x_hi, core, :, pl.ds(t * 512, 512)], sem[3 + t], sem[6 + t], x_mate
                    ))
            else:
                unfinished.append(send(
                    src.at[:, columns], whole.at[z, x_hi, core, :, columns], sem[3], sem[6], x_mate
                ))

        def forward(step):
            zz = lax.rem(z + 8 - step, 8)
            if step < 4:
                unfinished.append(send(block(zz), block(zz), sem[9 + step], sem[13 + step], z_next))

        def backward(step):
            zz = lax.rem(z + step, 8)
            if step < 3:
                unfinished.append(send(block(zz), block(zz), sem[17 + step], sem[20 + step], z_prev))

        def to_core(ref):
            send(ref, ref, sem[23], sem[24], sibling)

        def first():
            if name == "cq":
                for t in range(3):
                    part = whole.at[z, x_hi, core, :, pl.ds(t * 512, 512)]
                    pltpu.make_async_copy(part, part, sem[t]).wait()
                    arrived(whole.at[z, 1 - x_hi, core, :, pl.ds(t * 512, 512)], sem[3 + t], sem[6 + t], x_mate)
            else:
                part = whole.at[z, x_hi, core, :, columns]
                pltpu.make_async_copy(part, part, sem[0]).wait()
                arrived(whole.at[z, 1 - x_hi, core, :, columns], sem[3], sem[6], x_mate)
            forward(0)
            backward(0)
            if not last_y:
                to_core(block(z))

        def ring(step):
            zz = lax.rem(z + 8 - step, 8)
            arrived(block(zz), sem[9 + step - 1], sem[13 + step - 1], z_next)
            forward(step)
            if not last_y:
                to_core(block(zz))
            if step < 4:
                zz = lax.rem(z + step, 8)
                arrived(block(zz), sem[17 + step - 1], sem[20 + step - 1], z_prev)
                backward(step)
                if not last_y:
                    to_core(block(zz))

        def quarter(by, half=None):
            yy = lax.rem(y + 4 + by, 4)
            where = pl.ds(pl.multiple_of(yy * width, 128), width)
            if half is None:
                return whole.at[:, :, core, :, where]
            return whole.at[pl.ds(4 * half, 4), :, core, :, where]

        def along_y():
            unfinished.append(send(quarter(0), quarter(0), sem[25], sem[26], y_next))
            unfinished.append(send(quarter(0), quarter(0), sem[27], sem[28], y_prev))
            to_core(quarter(0))

        def along_y_second():
            arrived(quarter(-1), sem[25], sem[26], y_next)
            unfinished.append(send(quarter(-1, 0), quarter(-1, 0), sem[29], sem[5], y_next))
            to_core(quarter(-1))
            arrived(quarter(1), sem[27], sem[28], y_prev)
            unfinished.append(send(quarter(1, 1), quarter(1, 1), sem[7], sem[8], y_prev))
            to_core(quarter(1))

        def along_y_third():
            arrived(quarter(2, 0), sem[29], sem[5], y_next)
            arrived(quarter(2, 1), sem[7], sem[8], y_prev)
            to_core(quarter(2))

        def ready():
            arrived(whole.at[:, :, 1 - core], sem[23], sem[24], sibling)

        def sent():
            pltpu.make_async_remote_copy(
                src_ref=whole.at[:, :, core], dst_ref=whole.at[:, :, core], send_sem=sem[23], recv_sem=sem[24],
                device_id=sibling, device_id_type=MESH,
            ).wait_send()

        steps = [first] + [functools.partial(ring, s) for s in range(1, 5)]
        if last_y:
            steps += [along_y, along_y_second, along_y_third]
        return {"local": stage_local, "swap": stage_swap, "steps": steps, "ready": ready, "sent": sent}

    events = [weight_events(i) for i in range(6)]
    place = {spec[0]: i for i, spec in enumerate(WEIGHTS)}
    done = [0] * 6

    def advance(name, count=1):
        index = place[name]
        for _ in range(count):
            if done[index] < len(events[index]["steps"]):
                events[index]["steps"][done[index]]()
                done[index] += 1

    def finish(name):
        advance(name, 8)
        events[place[name]]["ready"]()

    def halo_send(number, table, rows_from, buffer, staging, devices):
        staging[...] = dot(table[...], rows_from).astype(BF16)
        for i, (at, count) in enumerate(PIECES):
            unfinished.append(send(
                staging.at[pl.ds(at, count)], buffer.at[pl.ds(NTOK + at, count)],
                halo_sems.at[number, i], halo_sems.at[number, 3 + i], devices[i],
            ))

    def halo_wait(number, buffer, devices):
        for i, (at, count) in enumerate(PIECES):
            arrived(buffer.at[pl.ds(NTOK + at, count)], halo_sems.at[number, i], halo_sems.at[number, 3 + i], devices[i])

    def pair_send(number, values, staging, buffer):
        staging[...] = jnp.concatenate([values, jnp.zeros((PAD - NMINE, values.shape[1]), F32)], axis=0).astype(BF16)
        unfinished.append(send(staging, buffer, pair_sems.at[number, 0], pair_sems.at[number, 1], pair_mate))

    def pair_wait(number, buffer):
        arrived(buffer, pair_sems.at[number, 0], pair_sems.at[number, 1], pair_mate)
        return buffer[...].astype(F32)[:NMINE]

    for event in events:
        event["local"]()
    barrier = pltpu.get_barrier_semaphore()
    for friend in friends:
        pl.semaphore_signal(barrier, inc=1, device_id=friend, device_id_type=MESH)
    xm = dot(to_merged[...], x_ref[...]).astype(BF16)
    xm_ref[...] = xm
    for buffer in (buf0, buf1, buf2, buf3):
        buffer[pl.ds(NTOK + HALO, NCAT - NTOK - HALO), :] = jnp.zeros((NCAT - NTOK - HALO, 512), BF16)
    buf0[pl.ds(0, NTOK), :] = xm
    pl.semaphore_wait(barrier, len(friends))
    for event in events[:2]:
        event["swap"]()
    halo_send(0, send_table, xm, buf0, sbuf0, behind)
    for event in events[2:]:
        event["swap"]()
    for _ in range(3):
        advance("fq")
        advance("fo")
    gm = dot(to_merged[...], g_ref[...]).astype(BF16)
    allowed = [dot(marks_ref[w], marks_ref[w], TRANS_B) for w in range(2)]
    advance("fq")
    advance("fo")
    halo_wait(0, buf0, behind)
    region = dot(region_table[...], buf0[...])
    unit, _ = normalise(region)
    region = (unit * gain_fine[...]).astype(BF16)
    advance("fq")
    advance("fo")
    advance("mw")
    advance("cq")
    advance("fq")
    advance("mw")
    advance("fq")
    advance("mw")
    advance("fq")
    finish("fq")

    def all_rows(ref, columns):
        value = ref[:, :, :, :, columns]
        return value.reshape(-1, value.shape[-1])

    for t in range(3):
        part = pl.ds(t * 512, 512)
        act[:, part] = dot(region, all_rows(fq, part)).astype(BF16)
    advance("cq")
    for w in range(2):
        attend_forward(act, mixed, chances, pl.ds(w * NWIN, NWIN), 8 * w, temper_fine, 0, allowed[w])
        advance("mw")
        advance("cq")
    finish("fo")
    delta = dot(mixed[...], all_rows(fo, slice(None))).astype(BF16)
    buf1[pl.ds(0, NTOK), :] = delta
    halo_send(1, halo_table, delta, buf1, sbuf1, ahead)
    advance("mw")
    advance("cq")
    advance("co")
    halo_wait(1, buf1, ahead)
    hidden = (xm_ref[...].astype(F32) + dot(back_table[...], buf1[...])).astype(BF16)
    hid[...] = hidden

    def cells(values):
        return jnp.concatenate([values[NMINE * i:NMINE * (i + 1)] for i in range(4)], axis=1)

    unit, merge_scale = normalise(cells(hidden.astype(F32)))
    wide_ref[...] = unit
    mn_ref[...] = (unit * gain_merge[...]).astype(BF16)
    finish("mw")

    def merge_step(n, carry):
        part = pl.ds(pl.multiple_of(n * 256, 256), 256)
        coarse_ref[:, part] = dot(mn_ref[...], all_rows(mw, part)).astype(BF16).astype(F32)
        return carry

    lax.fori_loop(0, 4, merge_step, 0)
    coarse = coarse_ref[...]
    coarse_unit, coarse_scale = normalise(coarse)
    coarse_norm = (coarse_unit * gain_coarse[...]).astype(BF16).astype(F32)
    pair_send(0, coarse_norm, psx, prx)
    advance("cq")
    advance("co")
    advance("sp")

    grad_cells = cells(gm.astype(F32)).astype(BF16)
    window = jnp.concatenate([coarse_norm, pair_wait(0, prx)], axis=0).astype(BF16)
    finish("cq")

    for t in range(3):
        part = pl.ds(t * 512, 512)
        cact[:, part] = dot(window, all_rows(cq, part)).astype(BF16)
    advance("co")
    advance("sp")
    attend_forward(cact, cmixed, cchances, pl.ds(0, NWIN), 0, temper_coarse, 8 * x_lo, None)
    advance("co")
    advance("sp")
    finish("co")
    co_mine = co[pl.ds(4 * x_lo, 4)].reshape(512, 1024)
    partial = dot(cmixed[...], co_mine)
    pair_send(1, partial[NMINE:], psy, pry)
    finish("sp")

    def grad_step(n, carry):
        rows = sp[pl.ds(2 * n, 2)].reshape(256, 2048)
        gnext_ref[:, pl.ds(pl.multiple_of(n * 256, 256), 256)] = dot(grad_cells, rows, TRANS_B).astype(BF16).astype(F32)
        return carry

    lax.fori_loop(0, 4, grad_step, 0)
    grad_next = gnext_ref[...]
    pair_send(2, grad_next, psz, prz)
    coarse_next = (coarse + (partial[:NMINE] + pair_wait(1, pry))).astype(BF16)
    cnext_ref[...] = coarse_next

    for q in range(4):
        part = pl.ds(q * 512, 512)
        rows = pl.ds(q * NMINE, NMINE)
        wide_part = dot(cnext_ref[...], all_rows(sp, part))
        gh_ref[rows, :] = hid[rows, :].astype(F32) + wide_part
    out_ref[...] = dot(from_merged[...], gh_ref[...].astype(BF16)).astype(BF16)

    grad_window = jnp.concatenate([grad_next, pair_wait(2, prz)], axis=0).astype(BF16)
    mixed[pl.ds(0, NWIN), :] = dot(grad_window, co_mine, TRANS_B).astype(BF16)
    attend_backward(cact, mixed, gact, cchances, pl.ds(0, NWIN), 0, temper_coarse, 8 * x_lo)
    grad_act = gact[pl.ds(0, NWIN), :]
    partial = jnp.concatenate(
        [dot(grad_act, cq[pl.ds(2 * n, 2)].reshape(256, 1536), TRANS_B) for n in range(4)], axis=1
    )
    pair_send(3, partial[NMINE:], psw, prw)
    grad_norm = (partial[:NMINE] + pair_wait(3, prw)).astype(BF16).astype(F32)
    grad_coarse = (grad_next + norm_back(grad_norm, gain_coarse[...], coarse_unit, coarse_scale)).astype(BF16)
    grad_merged = jnp.concatenate(
        [dot(grad_coarse, mw[n].reshape(256, 1024), TRANS_B) for n in range(8)], axis=1
    ).astype(BF16).astype(F32)
    grad_merged = norm_back(grad_merged, gain_merge[...], wide_ref[...], merge_scale).astype(BF16).astype(F32)
    for q in range(4):
        rows = pl.ds(q * NMINE, NMINE)
        gh_ref[rows, :] = grad_merged[:, q * 512:(q + 1) * 512]
    grad_hidden = (gm.astype(F32) + gh_ref[...]).astype(BF16)
    hid[...] = grad_hidden

    buf2[pl.ds(0, NTOK), :] = grad_hidden
    halo_send(2, send_table, grad_hidden, buf2, sbuf2, behind)
    halo_wait(2, buf2, behind)
    grad_region = dot(region_table[...], buf2[...]).astype(BF16)
    mixed[...] = dot(grad_region, all_rows(fo, slice(None)), TRANS_B).astype(BF16)
    for w in range(2):
        attend_backward(act, mixed, gact, chances, pl.ds(w * NWIN, NWIN), 8 * w, temper_fine, 0)
    grad_region = dot(gact[...], all_rows(fq, slice(None)), TRANS_B).astype(BF16)
    buf3[pl.ds(0, NTOK), :] = grad_region
    halo_send(3, halo_table, grad_region, buf3, sbuf3, ahead)
    unit, scale = normalise(xm_ref[...].astype(F32))
    halo_wait(3, buf3, ahead)
    grad_norm = dot(back_table[...], buf3[...]).astype(BF16).astype(F32)
    grad_in = hid[...].astype(F32) + norm_back(grad_norm, gain_fine[...], unit, scale)
    gin_ref[...] = dot(from_merged[...], grad_in.astype(BF16)).astype(BF16)

    for copy in unfinished:
        copy.wait_send()
    for event in events:
        event["sent"]()


def per_device(
    fine_tokens, grad_out, window_class, temper_fine, temper_coarse, gain_fine, fine_qkv, fine_out, gain_merge,
    merge_weight, gain_coarse, coarse_qkv, coarse_out, split_weight,
):
    at_pole = (lax.axis_index("lat") == lax.axis_size("lat") - 1) & (jnp.arange(ROWS) >= 3)
    labels = window_class + 3 * at_pole.astype(jnp.int32)[None, :, None]
    labels = labels.reshape(LEV, ROWS, 2, 12).transpose(2, 0, 1, 3).reshape(2, NWIN)
    marks = (labels[:, :, None] == jnp.arange(128)[None, None, :]).astype(BF16)
    vmem = pl.BlockSpec(memory_space=pltpu.VMEM)
    smem = pl.BlockSpec(memory_space=pltpu.SMEM)
    anyplace = pl.BlockSpec(memory_space=pl.ANY)
    scratch = [pltpu.VMEM((8, 2, 2, rows, cols), BF16) for _, rows, cols, _ in WEIGHTS]
    scratch += [pltpu.VMEM((NCAT, 512), BF16)] * 4 + [pltpu.VMEM((HALO, 512), BF16)] * 4
    scratch += [pltpu.VMEM((PAD, 1024), BF16)] * 8
    scratch += [
        pltpu.VMEM((NTOK, 512), BF16),
        pltpu.VMEM((NTOK, 1536), BF16),
        pltpu.VMEM((NTOK, 512), BF16),
        pltpu.VMEM((NTOK, 1536), BF16),
        pltpu.VMEM((16, NWIN, NWIN), F32),
        pltpu.VMEM((NTOK, 512), BF16),
        pltpu.VMEM((NWIN, 1536), BF16),
        pltpu.VMEM((NWIN, 512), BF16),
        pltpu.VMEM((8, NWIN, NWIN), F32),
        pltpu.VMEM((NMINE, 1024), F32),
        pltpu.VMEM((NMINE, 1024), BF16),
        pltpu.VMEM((NMINE, 1024), F32),
        pltpu.VMEM((NMINE, 2048), BF16),
        pltpu.VMEM((NMINE, 2048), F32),
        pltpu.VMEM((NTOK, 512), F32),
        pltpu.SemaphoreType.DMA((6, SEMS_PER_WEIGHT)),
        pltpu.SemaphoreType.DMA((4, 6)),
        pltpu.SemaphoreType.DMA((4, 2)),
    ]
    tables = layout_tables()
    output, grad_in = pl.pallas_call(
        kernel,
        out_shape=[jax.ShapeDtypeStruct((NTOK, 512), BF16)] * 2,
        in_specs=[vmem] * 3 + [smem] * 2 + [vmem] * 3 + [anyplace] * 6 + [vmem] * 6,
        out_specs=[vmem] * 2,
        scratch_shapes=scratch,
        compiler_params=pltpu.CompilerParams(
            collective_id=0, has_side_effects=True, vmem_limit_bytes=56 * 1024 * 1024
        ),
    )(
        fine_tokens.reshape(NTOK, 512), grad_out.reshape(NTOK, 512), marks, temper_fine, temper_coarse,
        gain_fine.reshape(1, -1), gain_merge.reshape(1, -1), gain_coarse.reshape(1, -1),
        fine_qkv, fine_out, merge_weight, coarse_qkv, coarse_out, split_weight, *tables,
    )
    return output.reshape(fine_tokens.shape), grad_in.reshape(fine_tokens.shape)


def solution(mesh):
    tiles = P(None, "lat", "lon", None)
    shards = P("lon", None)
    return jax.shard_map(
        per_device,
        mesh=mesh,
        in_specs=(
            tiles, tiles, P(None, "lat", "lon"), P(), P(), P(), shards, shards, P(), shards, P(), shards, shards, shards,
        ),
        out_specs=(tiles, tiles),
        check_vma=False,
    )
```

time: 585 us -> 172 us (0.29); the launches traced: 574 us -> 169 us
  waiting for transfers between devices: 332 us -> 0 us
  Pallas kernels: 0 us -> 164 us
  local copies, waits for them, and re-layouts: 88.5 us -> 3.31 us
  blocking collectives: 41.2 us -> 0 us
  matrix products: 40.7 us -> 0 us
  other arithmetic: 35.2 us -> 0.82 us
  starting transfers between devices: 21.2 us -> 0 us
  between operations: 15.6 us -> 0.67 us
    all_gather x5 -> x0, waiting for transfers between devices: 296 us -> none  [the longest x1 84.1 us: per_device(): lax.all_gather(coarse_qkv, 'lon', axis=0, tiled=True)]
    pallas_call x0 -> x1, Pallas kernels: none -> 164 us  [per_device(): pl.pallas_call(kernel, out_shape=[jax.ShapeDtypeStruct((NTOK, 512), BF16)...]
    all_gather x1 -> x0, blocking collectives: 41.2 us -> none  [per_device(): lax.all_gather(fine_out, 'lon', axis=0, tiled=True)]
    dot_general x24 -> x0, matrix products: 40.7 us -> none  [the longest x2 7.66 us: merge_section(): jnp.dot(merged_norm.reshape(-1, merged_norm.shape[3]), weight_all, prefer...]
    ppermute x16 -> x0, waiting for transfers between devices: 32.4 us -> none  [the longest x8 30.3 us: from_behind(): lax.ppermute(shard, axis, [(i, (i + by) % devices) for i in range(devices)])]
    ppermute x16 -> x0, starting transfers between devices: 21 us -> none  [the longest x8 17.6 us: from_behind(): lax.ppermute(shard, axis, [(i, (i + by) % devices) for i in range(devices)])]
    unnamed x134 -> x6, local copies, waits for them, and re-layouts: 18.3 us -> 3.13 us
    another operation x9 -> x0, local copies, waits for them, and re-layouts: 12.9 us -> none
  transfers between devices with their start and end apart: 21 -> 0, of which waited for: 13 -> 0; matrix products, arithmetic and copies ran while one was open for 20% -> 0% of each run, Pallas kernels for 0% -> 0%
where the time goes in v1:
time: 172 us; the launch traced here: 169 us
  Pallas kernels  164 us (95%)
  local copies, waits for them, and re-layouts  3.31 us (2%)
    pallas_call x1, Pallas kernels, per_device(): pl.pallas_call(kernel, out_shape=[jax.ShapeDtypeStruct((NTOK, 512), BF16)...  164 us

profile of v1, /device:TPU:0, one launch (start us, length us, event | category | flops | bytes accessed | tf_op | source)
XLA Modules:
  0.0 168.6 jit_solution(17670213250857887823)
XLA Ops:
  0.6 0.0 copy-start.1
  0.7 0.7 copy-done.1
  1.3 0.1 broadcast_add_fusion
  1.4 0.1 reshape.38
  1.5 0.1 eq.19
  1.6 0.7 fusion.marks_ref
  2.3 163.8 %shard_map.203 = (bf16[288,512]{1,0:T(8,128)(2,1)}, bf16[288,512]{1,0:T(8,128)(2,1)}) custom-call(bf16[288,512]{1,0:T(8,128)(2,1)} %bitcast.14, bf16[288,512]{1,0:T(8,128)(2,1)} %bitcast.15, bf16[2,144,128]{2,1,0:T(8,128)(2,1)} %fusion.marks_ref, f32[8]{0:T(128)} %temper_fine.1, f32[16]{0:T(128)} %temper_coarse.1, f32[1,512]{1,0:T(1,128)} %bitcast.19, ...), custom_call_target="tpu_custom_call" | custom-call | tf_op jit(solution)/shard_map/pallas_call | solution.py:555
  166.2 0.0 copy-start
  166.2 1.7 %copy.28 = bf16[2,6,24,512]{3,2,1,0:T(8,128)(2,1)} copy(bf16[2,6,24,512]{3,2,1,0:T(8,128)(2,1)} %bitcast.13) | data formatting | bytes 589824
  167.9 0.0 copy-done
  167.9 0.7 copy.29
  (2 shorter events, 0.0 us)
Async XLA Ops:
  0.6 0.7 copy-start.1
  166.2 1.8 %copy-start = (bf16[288,512]{1,0:T(8,128)(2,1)S(1)}, bf16[288,512]{1,0:T(8,128)(2,1)}, u32[]{:S(2)}) copy-start(bf16[288,512]{1,0:T(8,128)(2,1)} %get-tuple-element.5) | copy-start | bytes 884740

commit v2 on v1

--- a/solution.py
+++ b/solution.py
@@ -93,13 +93,17 @@
     return jnp.where(low, first, second)
 
 
-def attend_forward(act, mixed, chances, rows, first, temper, temper_at, allowed):
+def head_columns(p, heads):
+    first, step, kind = heads
+    return [pl.ds(pl.multiple_of(first + p * step + t * kind, 128), 128) for t in range(3)]
+
+
+def attend_forward(act, mixed, chances, rows, first, temper, temper_at, allowed, heads, start, stop):
     low = half_mask(NWIN)
 
     def pair(p, carry):
-        q = act[rows, pl.ds(pl.multiple_of(p * 128, 128), 128)].astype(F32)
-        k = act[rows, pl.ds(pl.multiple_of(p * 128 + 512, 128), 128)].astype(F32)
-        v = act[rows, pl.ds(pl.multiple_of(p * 128 + 1024, 128), 128)]
+        q, k, v = (act[rows, s] for s in head_columns(p, heads))
+        q, k = q.astype(F32), k.astype(F32)
         q = q * lax.rsqrt(half_sums(q * q, low) + UNIT_EPS)
         k = (k * lax.rsqrt(half_sums(k * k, low) + UNIT_EPS)).astype(BF16)
         mixes = []
@@ -115,20 +119,20 @@
         mixed[rows, pl.ds(pl.multiple_of(p * 128, 128), 128)] = jnp.where(low, mixes[0], mixes[1]).astype(BF16)
         return carry
 
-    lax.fori_loop(0, 4, pair, 0)
-
-
-def attend_backward(act, grad_mixed, grad_act, chances, rows, first, temper, temper_at):
+    lax.fori_loop(start, stop, pair, 0)
+
+
+def attend_backward(act, grad_mixed, grad_act, chances, rows, first, temper, temper_at, heads):
     low = half_mask(NWIN)
 
     def pair(p, carry):
-        at = [pl.ds(pl.multiple_of(p * 128 + 512 * t, 128), 128) for t in range(3)]
+        at = head_columns(p, heads)
         q, k, v = (act[rows, s].astype(F32) for s in at)
         q_scale = lax.rsqrt(half_sums(q * q, low) + UNIT_EPS)
         k_scale = lax.rsqrt(half_sums(k * k, low) + UNIT_EPS)
         q, k = q * q_scale, k * k_scale
         q_low, k_low = q.astype(BF16), k.astype(BF16)
-        grad = grad_mixed[rows, at[0]]
+        grad = grad_mixed[rows, pl.ds(pl.multiple_of(p * 128, 128), 128)]
         gq, gk, gv = [], [], []
         for j in range(2):
             mine = low if j == 0 else jnp.logical_not(low)
@@ -149,14 +153,19 @@
 
 
 WEIGHTS = (
-    ("fq", 16, 1536, True),
-    ("fo", 16, 512, False),
-    ("mw", 64, 1024, True),
-    ("cq", 32, 1536, False),
-    ("co", 32, 1024, False),
-    ("sp", 32, 2048, True),
+    ("fk", 16, 512, "x", 512),
+    ("fo", 16, 512, "x", 0),
+    ("fq", 16, 512, "y", 0),
+    ("fv", 16, 512, "y", 1024),
+    ("mwa", 64, 512, "x", 0),
+    ("mwb", 64, 512, "y", 512),
+    ("cq", 32, 1536, "z", None),
+    ("co", 32, 1024, "x", 0),
+    ("spa", 32, 1024, "x", 0),
+    ("spb", 32, 1024, "y", 1024),
 )
-SEMS_PER_WEIGHT = 30
+FINE = ("fk", "fo", "fq", "fv")
+SEMS_PER_WEIGHT = 33
 
 
 def kernel(
@@ -164,7 +173,7 @@
     fq_in, fo_in, mw_in, cq_in, co_in, sp_in,
     to_merged, from_merged, send_table, region_table, back_table, halo_table,
     out_ref, gin_ref,
-    fq, fo, mw, cq, co, sp,
+    fk, fo, fq, fv, mwa, mwb, cq, co, spa, spb,
     buf0, buf1, buf2, buf3, sbuf0, sbuf1, sbuf2, sbuf3,
     prx, pry, prz, prw, psx, psy, psz, psw,
     xm_ref, act, mixed, gact, chances, hid, cact, cmixed, cchances, coarse_ref, cnext_ref, gnext_ref, mn_ref, wide_ref, gh_ref,
@@ -182,12 +191,20 @@
 
     z_next, z_prev = (lat, at_lon(4)), (lat, at_lon(-4))
     y_next, y_prev = (at_lat(2), lon), (at_lat(-2), lon)
+    x = 2 * x_hi + x_lo
+
+    def at_x(by):
+        there = lax.rem(x + 4 + by, 4)
+        return (2 * y + lax.rem(there, 2), 4 * z + 2 * (there // 2) + core)
+
+    x_next, x_prev = at_x(1), at_x(-1)
     x_mate = (lat + 1 - 2 * x_lo, lon + 2 - 4 * x_hi)
     sibling = (lat, lon + 1 - 2 * core)
     pair_mate = (lat + 1 - 2 * x_lo, lon)
     behind = ((at_lat(-1), lon), (lat, at_lon(-1)), (at_lat(-1), at_lon(-1)))
     ahead = ((at_lat(1), lon), (lat, at_lon(1)), (at_lat(1), at_lon(1)))
-    friends = (z_next, z_prev, y_next, y_prev, x_mate) + behind + ahead
+    z_all = tuple((lat, at_lon(4 * by)) for by in range(1, 8))
+    friends = z_all + (y_next, y_prev, x_next, x_prev, x_mate) + behind + ahead
 
     unfinished = []
 
@@ -203,42 +220,49 @@
             src_ref=dst, dst_ref=dst, send_sem=sem_out, recv_sem=sem_in, device_id=device, device_id_type=MESH
         ).wait_recv()
 
-    inputs = {"fq": fq_in, "fo": fo_in, "mw": mw_in, "cq": cq_in, "co": co_in, "sp": sp_in}
-    buffers = {"fq": fq, "fo": fo, "mw": mw, "cq": cq, "co": co, "sp": sp}
+    inputs = (fq_in, fo_in, fq_in, fq_in, mw_in, mw_in, cq_in, co_in, sp_in, sp_in)
+    buffers = (fk, fo, fq, fv, mwa, mwb, cq, co, spa, spb)
 
     def weight_events(index):
-        name, rows, cols, last_y = WEIGHTS[index]
-        src, whole = inputs[name], buffers[name]
-        width = cols // 4 if last_y else cols
-        if last_y:
-            columns = pl.ds(pl.multiple_of(y * width, 128), width)
-        else:
-            columns = slice(None)
+        name, rows, cols, axis, base = WEIGHTS[index]
+        src, whole = inputs[index], buffers[index]
+        by_x, by_z = axis == "x", axis == "z"
+        width = {"x": cols // 2, "y": cols // 4, "z": cols}[axis]
+        at, after, before = (x, x_next, x_prev) if by_x else (y, y_next, y_prev)
         sem = [sems.at[index, i] for i in range(SEMS_PER_WEIGHT)]
 
+        def lanes(part):
+            return pl.ds(pl.multiple_of(part * width, 128), width)
+
+        def piece(by, levels):
+            there = lax.rem(at + 4 + by, 4)
+            if by_z:
+                return whole.at[levels, :, core]
+            if by_x:
+                return whole.at[levels, there // 2, core, :, lanes(lax.rem(there, 2))]
+            return whole.at[levels, :, core, :, lanes(there)]
+
         def block(zz):
-            return whole.at[zz, :, core, :, columns]
+            return piece(0, zz)
+
+        def source(parity):
+            if by_z:
+                return [
+                    (pl.ds(pl.multiple_of(t * 1024 + parity * 512, 128), 512), pl.ds(t * 512, 512)) for t in range(3)
+                ]
+            part = x_lo if by_x else y
+            return [(pl.ds(pl.multiple_of(base + part * width, 128), width), lanes(part))]
 
         def stage_local():
-            if name == "cq":
-                for t in range(3):
-                    from_at = pl.ds(pl.multiple_of(t * 1024 + x_lo * 512, 128), 512)
-                    pltpu.make_async_copy(
-                        src.at[:, from_at], whole.at[z, x_hi, core, :, pl.ds(t * 512, 512)], sem[t]
-                    ).start()
-            else:
-                pltpu.make_async_copy(src.at[:, columns], whole.at[z, x_hi, core, :, columns], sem[0]).start()
+            for t, (from_at, to_at) in enumerate(source(x_lo)):
+                pltpu.make_async_copy(src.at[:, from_at], whole.at[z, x_hi, core, :, to_at], sem[t]).start()
 
         def stage_swap():
-            if name == "cq":
-                for t in range(3):
-                    from_at = pl.ds(pl.multiple_of(t * 1024 + (1 - x_lo) * 512, 128), 512)
-                    unfinished.append(send(
-                        src.at[:, from_at], whole.at[z, x_hi, core, :, pl.ds(t * 512, 512)], sem[3 + t], sem[6 + t], x_mate
-                    ))
-            else:
+            if by_x:
+                return
+            for t, (from_at, to_at) in enumerate(source(1 - x_lo)):
                 unfinished.append(send(
-                    src.at[:, columns], whole.at[z, x_hi, core, :, columns], sem[3], sem[6], x_mate
+                    src.at[:, from_at], whole.at[z, x_hi, core, :, to_at], sem[3 + t], sem[6 + t], x_mate
                 ))
 
         def forward(step):
@@ -255,57 +279,62 @@
             send(ref, ref, sem[23], sem[24], sibling)
 
         def first():
-            if name == "cq":
-                for t in range(3):
-                    part = whole.at[z, x_hi, core, :, pl.ds(t * 512, 512)]
-                    pltpu.make_async_copy(part, part, sem[t]).wait()
-                    arrived(whole.at[z, 1 - x_hi, core, :, pl.ds(t * 512, 512)], sem[3 + t], sem[6 + t], x_mate)
-            else:
-                part = whole.at[z, x_hi, core, :, columns]
-                pltpu.make_async_copy(part, part, sem[0]).wait()
-                arrived(whole.at[z, 1 - x_hi, core, :, columns], sem[3], sem[6], x_mate)
+            for t, (from_at, to_at) in enumerate(source(x_lo)):
+                part = whole.at[z, x_hi, core, :, to_at]
+                pltpu.make_async_copy(part, part, sem[t]).wait()
+                if not by_x:
+                    arrived(whole.at[z, 1 - x_hi, core, :, to_at], sem[3 + t], sem[6 + t], x_mate)
+            if name in FINE:
+                for by in (4, 3, 5, 2, 6, 1, 7):
+                    unfinished.append(send(block(z), block(z), sem[8 + by], sem[15 + by], (lat, at_lon(4 * by))))
+                return
             forward(0)
             backward(0)
-            if not last_y:
+            if by_z:
                 to_core(block(z))
+
+        def along():
+            mine = piece(0, slice(None))
+            unfinished.append(send(mine, mine, sem[25], sem[26], after))
+            unfinished.append(send(mine, mine, sem[27], sem[28], before))
+            to_core(mine)
+
+        def collect():
+            for by in (1, 7, 2, 6, 3, 5, 4):
+                arrived(block(lax.rem(z + 8 - by, 8)), sem[8 + by], sem[15 + by], z_next)
+            along()
 
         def ring(step):
             zz = lax.rem(z + 8 - step, 8)
             arrived(block(zz), sem[9 + step - 1], sem[13 + step - 1], z_next)
             forward(step)
-            if not last_y:
+            if by_z:
                 to_core(block(zz))
             if step < 4:
                 zz = lax.rem(z + step, 8)
                 arrived(block(zz), sem[17 + step - 1], sem[20 + step - 1], z_prev)
                 backward(step)
-                if not last_y:
+                if by_z:
                     to_core(block(zz))
-
-        def quarter(by, half=None):
-            yy = lax.rem(y + 4 + by, 4)
-            where = pl.ds(pl.multiple_of(yy * width, 128), width)
-            if half is None:
-                return whole.at[:, :, core, :, where]
-            return whole.at[pl.ds(4 * half, 4), :, core, :, where]
-
-        def along_y():
-            unfinished.append(send(quarter(0), quarter(0), sem[25], sem[26], y_next))
-            unfinished.append(send(quarter(0), quarter(0), sem[27], sem[28], y_prev))
-            to_core(quarter(0))
-
-        def along_y_second():
-            arrived(quarter(-1), sem[25], sem[26], y_next)
-            unfinished.append(send(quarter(-1, 0), quarter(-1, 0), sem[29], sem[5], y_next))
-            to_core(quarter(-1))
-            arrived(quarter(1), sem[27], sem[28], y_prev)
-            unfinished.append(send(quarter(1, 1), quarter(1, 1), sem[7], sem[8], y_prev))
-            to_core(quarter(1))
-
-        def along_y_third():
-            arrived(quarter(2, 0), sem[29], sem[5], y_next)
-            arrived(quarter(2, 1), sem[7], sem[8], y_prev)
-            to_core(quarter(2))
+            elif not by_z:
+                along()
+
+        low, high = pl.ds(0, 4), pl.ds(4, 4)
+
+        def second():
+            theirs = piece(-1, slice(None))
+            arrived(theirs, sem[25], sem[26], after)
+            unfinished.append(send(piece(-1, low), piece(-1, low), sem[29], sem[30], after))
+            to_core(theirs)
+            theirs = piece(1, slice(None))
+            arrived(theirs, sem[27], sem[28], before)
+            unfinished.append(send(piece(1, high), piece(1, high), sem[31], sem[32], before))
+            to_core(theirs)
+
+        def third():
+            arrived(piece(2, low), sem[29], sem[30], after)
+            arrived(piece(2, high), sem[31], sem[32], before)
+            to_core(piece(2, slice(None)))
 
         def ready():
             arrived(whole.at[:, :, 1 - core], sem[23], sem[24], sibling)
@@ -316,25 +345,28 @@
                 device_id=sibling, device_id_type=MESH,
             ).wait_send()
 
-        steps = [first] + [functools.partial(ring, s) for s in range(1, 5)]
-        if last_y:
-            steps += [along_y, along_y_second, along_y_third]
+        steps = [first] + ([collect] if name in FINE else [functools.partial(ring, s) for s in range(1, 5)])
+        if not by_z:
+            steps += [second, third]
         return {"local": stage_local, "swap": stage_swap, "steps": steps, "ready": ready, "sent": sent}
 
-    events = [weight_events(i) for i in range(6)]
+    events = [weight_events(i) for i in range(len(WEIGHTS))]
     place = {spec[0]: i for i, spec in enumerate(WEIGHTS)}
-    done = [0] * 6
-
-    def advance(name, count=1):
-        index = place[name]
-        for _ in range(count):
+    done = [0] * len(WEIGHTS)
+
+    def advance(*names):
+        for name in names:
+            index = place[name]
             if done[index] < len(events[index]["steps"]):
                 events[index]["steps"][done[index]]()
                 done[index] += 1
 
-    def finish(name):
-        advance(name, 8)
-        events[place[name]]["ready"]()
+    def finish(*names):
+        for name in names:
+            while done[place[name]] < len(events[place[name]]["steps"]):
+                advance(name)
+        for name in names:
+            events[place[name]]["ready"]()
 
     def halo_send(number, table, rows_from, buffer, staging, devices):
         staging[...] = dot(table[...], rows_from).astype(BF16)
@@ -367,55 +399,49 @@
         buffer[pl.ds(NTOK + HALO, NCAT - NTOK - HALO), :] = jnp.zeros((NCAT - NTOK - HALO, 512), BF16)
     buf0[pl.ds(0, NTOK), :] = xm
     pl.semaphore_wait(barrier, len(friends))
-    for event in events[:2]:
+    for event in events[:4]:
         event["swap"]()
     halo_send(0, send_table, xm, buf0, sbuf0, behind)
-    for event in events[2:]:
+    for event in events[4:]:
         event["swap"]()
-    for _ in range(3):
-        advance("fq")
-        advance("fo")
+    advance(*FINE)
     gm = dot(to_merged[...], g_ref[...]).astype(BF16)
     allowed = [dot(marks_ref[w], marks_ref[w], TRANS_B) for w in range(2)]
-    advance("fq")
-    advance("fo")
+    advance(*FINE)
+    advance("mwa", "mwb")
     halo_wait(0, buf0, behind)
     region = dot(region_table[...], buf0[...])
     unit, _ = normalise(region)
     region = (unit * gain_fine[...]).astype(BF16)
-    advance("fq")
-    advance("fo")
-    advance("mw")
-    advance("cq")
-    advance("fq")
-    advance("mw")
-    advance("fq")
-    advance("mw")
-    advance("fq")
-    finish("fq")
-
-    def all_rows(ref, columns):
+    advance(*FINE)
+    advance("mwa", "mwb")
+    advance(*FINE)
+    advance("mwa", "mwb", "cq")
+    finish("fq", "fk", "fv")
+
+    def all_rows(ref, columns=slice(None)):
         value = ref[:, :, :, :, columns]
         return value.reshape(-1, value.shape[-1])
 
-    for t in range(3):
-        part = pl.ds(t * 512, 512)
-        act[:, part] = dot(region, all_rows(fq, part)).astype(BF16)
-    advance("cq")
+    for t, weight in enumerate((fq, fk, fv)):
+        act[:, pl.ds(t * 512, 512)] = dot(region, all_rows(weight)).astype(BF16)
+    advance("mwa", "mwb")
+    heads = (0, 128, 512)
+    then = (("mwa", "mwb", "co"), ("cq",), ("co",), ("cq", "spa", "spb"))
     for w in range(2):
-        attend_forward(act, mixed, chances, pl.ds(w * NWIN, NWIN), 8 * w, temper_fine, 0, allowed[w])
-        advance("mw")
-        advance("cq")
+        rows = pl.ds(w * NWIN, NWIN)
+        for half in range(2):
+            attend_forward(act, mixed, chances, rows, 8 * w, temper_fine, 0, allowed[w], heads, 2 * half, 2 * half + 2)
+            advance(*then[2 * w + half])
     finish("fo")
-    delta = dot(mixed[...], all_rows(fo, slice(None))).astype(BF16)
+    delta = dot(mixed[...], all_rows(fo)).astype(BF16)
     buf1[pl.ds(0, NTOK), :] = delta
     halo_send(1, halo_table, delta, buf1, sbuf1, ahead)
-    advance("mw")
-    advance("cq")
-    advance("co")
+    advance("mwa", "mwb", "co", "spa", "spb", "cq")
     halo_wait(1, buf1, ahead)
     hidden = (xm_ref[...].astype(F32) + dot(back_table[...], buf1[...])).astype(BF16)
     hid[...] = hidden
+    advance("mwa", "mwb", "co", "spa", "spb")
 
     def cells(values):
         return jnp.concatenate([values[NMINE * i:NMINE * (i + 1)] for i in range(4)], axis=1)
@@ -423,70 +449,75 @@
     unit, merge_scale = normalise(cells(hidden.astype(F32)))
     wide_ref[...] = unit
     mn_ref[...] = (unit * gain_merge[...]).astype(BF16)
-    finish("mw")
-
-    def merge_step(n, carry):
-        part = pl.ds(pl.multiple_of(n * 256, 256), 256)
-        coarse_ref[:, part] = dot(mn_ref[...], all_rows(mw, part)).astype(BF16).astype(F32)
-        return carry
-
-    lax.fori_loop(0, 4, merge_step, 0)
+    finish("mwa", "mwb")
+
+    for n, weight in enumerate((mwa, mwb)):
+        for half in range(2):
+            part = pl.ds(half * 256, 256)
+            coarse_ref[:, pl.ds(n * 512 + half * 256, 256)] = dot(mn_ref[...], all_rows(weight, part)).astype(BF16).astype(F32)
+    advance("cq", "co", "spa", "spb")
     coarse = coarse_ref[...]
     coarse_unit, coarse_scale = normalise(coarse)
     coarse_norm = (coarse_unit * gain_coarse[...]).astype(BF16).astype(F32)
     pair_send(0, coarse_norm, psx, prx)
-    advance("cq")
-    advance("co")
-    advance("sp")
-
+    advance("spa", "spb", "co")
     grad_cells = cells(gm.astype(F32)).astype(BF16)
-    window = jnp.concatenate([coarse_norm, pair_wait(0, prx)], axis=0).astype(BF16)
     finish("cq")
-
+    mine = [dot(coarse_norm.astype(BF16), all_rows(cq, pl.ds(t * 512, 512))) for t in range(3)]
+    theirs = pair_wait(0, prx).astype(BF16)
     for t in range(3):
         part = pl.ds(t * 512, 512)
-        cact[:, part] = dot(window, all_rows(cq, part)).astype(BF16)
-    advance("co")
-    advance("sp")
-    attend_forward(cact, cmixed, cchances, pl.ds(0, NWIN), 0, temper_coarse, 8 * x_lo, None)
-    advance("co")
-    advance("sp")
+        cact[:, part] = jnp.concatenate([mine[t], dot(theirs, all_rows(cq, part))], axis=0).astype(BF16)
+    for half in range(2):
+        attend_forward(
+            cact, cmixed, cchances, pl.ds(0, NWIN), 0, temper_coarse, 8 * x_lo, None, heads, 2 * half, 2 * half + 2
+        )
+        advance("co", "spa", "spb")
     finish("co")
     co_mine = co[pl.ds(4 * x_lo, 4)].reshape(512, 1024)
-    partial = dot(cmixed[...], co_mine)
-    pair_send(1, partial[NMINE:], psy, pry)
-    finish("sp")
+    mix = cmixed[...].astype(F32)
+    pair_send(1, dot(mix[NMINE:].astype(BF16), co_mine), psy, pry)
+    partial = dot(mix[:NMINE].astype(BF16), co_mine)
+    finish("spa", "spb")
 
     def grad_step(n, carry):
-        rows = sp[pl.ds(2 * n, 2)].reshape(256, 2048)
-        gnext_ref[:, pl.ds(pl.multiple_of(n * 256, 256), 256)] = dot(grad_cells, rows, TRANS_B).astype(BF16).astype(F32)
+        total = dot(grad_cells[:, :1024], spa[pl.ds(2 * n, 2)].reshape(256, 1024), TRANS_B)
+        total += dot(grad_cells[:, 1024:], spb[pl.ds(2 * n, 2)].reshape(256, 1024), TRANS_B)
+        gnext_ref[:, pl.ds(pl.multiple_of(n * 256, 256), 256)] = total.astype(BF16).astype(F32)
         return carry
 
     lax.fori_loop(0, 4, grad_step, 0)
     grad_next = gnext_ref[...]
     pair_send(2, grad_next, psz, prz)
-    coarse_next = (coarse + (partial[:NMINE] + pair_wait(1, pry))).astype(BF16)
+    coarse_next = (coarse + (partial + pair_wait(1, pry))).astype(BF16)
     cnext_ref[...] = coarse_next
 
     for q in range(4):
-        part = pl.ds(q * 512, 512)
+        part = pl.ds(q % 2 * 512, 512)
         rows = pl.ds(q * NMINE, NMINE)
-        wide_part = dot(cnext_ref[...], all_rows(sp, part))
+        wide_part = dot(cnext_ref[...], all_rows((spa, spb)[q // 2], part))
         gh_ref[rows, :] = hid[rows, :].astype(F32) + wide_part
     out_ref[...] = dot(from_merged[...], gh_ref[...].astype(BF16)).astype(BF16)
 
     grad_window = jnp.concatenate([grad_next, pair_wait(2, prz)], axis=0).astype(BF16)
     mixed[pl.ds(0, NWIN), :] = dot(grad_window, co_mine, TRANS_B).astype(BF16)
-    attend_backward(cact, mixed, gact, cchances, pl.ds(0, NWIN), 0, temper_coarse, 8 * x_lo)
-    grad_act = gact[pl.ds(0, NWIN), :]
-    partial = jnp.concatenate(
-        [dot(grad_act, cq[pl.ds(2 * n, 2)].reshape(256, 1536), TRANS_B) for n in range(4)], axis=1
-    )
-    pair_send(3, partial[NMINE:], psw, prw)
-    grad_norm = (partial[:NMINE] + pair_wait(3, prw)).astype(BF16).astype(F32)
+    attend_backward(cact, mixed, gact, cchances, pl.ds(0, NWIN), 0, temper_coarse, 8 * x_lo, heads)
+    grad_act = gact[pl.ds(0, NWIN), :].astype(F32)
+
+    def through_cq(rows):
+        return jnp.concatenate([dot(rows, cq[pl.ds(2 * n, 2)].reshape(256, 1536), TRANS_B) for n in range(4)], axis=1)
+
+    pair_send(3, through_cq(grad_act[NMINE:].astype(BF16)), psw, prw)
+    partial = through_cq(grad_act[:NMINE].astype(BF16))
+    grad_norm = (partial + pair_wait(3, prw)).astype(BF16).astype(F32)
     grad_coarse = (grad_next + norm_back(grad_norm, gain_coarse[...], coarse_unit, coarse_scale)).astype(BF16)
     grad_merged = jnp.concatenate(
-        [dot(grad_coarse, mw[n].reshape(256, 1024), TRANS_B) for n in range(8)], axis=1
+        [
+            dot(grad_coarse[:, :512], mwa[n].reshape(256, 512), TRANS_B)
+            + dot(grad_coarse[:, 512:], mwb[n].reshape(256, 512), TRANS_B)
+            for n in range(8)
+        ],
+        axis=1,
     ).astype(BF16).astype(F32)
     grad_merged = norm_back(grad_merged, gain_merge[...], wide_ref[...], merge_scale).astype(BF16).astype(F32)
     for q in range(4):
@@ -499,10 +530,12 @@
     halo_send(2, send_table, grad_hidden, buf2, sbuf2, behind)
     halo_wait(2, buf2, behind)
     grad_region = dot(region_table[...], buf2[...]).astype(BF16)
-    mixed[...] = dot(grad_region, all_rows(fo, slice(None)), TRANS_B).astype(BF16)
+    mixed[...] = dot(grad_region, all_rows(fo), TRANS_B).astype(BF16)
     for w in range(2):
-        attend_backward(act, mixed, gact, chances, pl.ds(w * NWIN, NWIN), 8 * w, temper_fine, 0)
-    grad_region = dot(gact[...], all_rows(fq, slice(None)), TRANS_B).astype(BF16)
+        attend_backward(act, mixed, gact, chances, pl.ds(w * NWIN, NWIN), 8 * w, temper_fine, 0, heads)
+    grad_region = sum(
+        dot(gact[:, pl.ds(t * 512, 512)], all_rows(weight), TRANS_B) for t, weight in enumerate((fq, fk, fv))
+    ).astype(BF16)
     buf3[pl.ds(0, NTOK), :] = grad_region
     halo_send(3, halo_table, grad_region, buf3, sbuf3, ahead)
     unit, scale = normalise(xm_ref[...].astype(F32))
@@ -528,7 +561,7 @@
     vmem = pl.BlockSpec(memory_space=pltpu.VMEM)
     smem = pl.BlockSpec(memory_space=pltpu.SMEM)
     anyplace = pl.BlockSpec(memory_space=pl.ANY)
-    scratch = [pltpu.VMEM((8, 2, 2, rows, cols), BF16) for _, rows, cols, _ in WEIGHTS]
+    scratch = [pltpu.VMEM((8, 2, 2, rows, cols), BF16) for _, rows, cols, _, _ in WEIGHTS]
     scratch += [pltpu.VMEM((NCAT, 512), BF16)] * 4 + [pltpu.VMEM((HALO, 512), BF16)] * 4
     scratch += [pltpu.VMEM((PAD, 1024), BF16)] * 8
     scratch += [
@@ -547,7 +580,7 @@
         pltpu.VMEM((NMINE, 2048), BF16),
         pltpu.VMEM((NMINE, 2048), F32),
         pltpu.VMEM((NTOK, 512), F32),
-        pltpu.SemaphoreType.DMA((6, SEMS_PER_WEIGHT)),
+        pltpu.SemaphoreType.DMA((len(WEIGHTS), SEMS_PER_WEIGHT)),
         pltpu.SemaphoreType.DMA((4, 6)),
         pltpu.SemaphoreType.DMA((4, 2)),
     ]

time: 172 us -> 132 us (0.77)
  Pallas kernels: 164 us -> 125 us
    pallas_call x1, Pallas kernels: 164 us -> 125 us  [per_device(): pl.pallas_call(kernel, out_shape=[jax.ShapeDtypeStruct((NTOK, 512), BF16)...]
where the time goes in v2:
time: 132 us; the launch traced here: 129 us
  Pallas kernels  125 us (95%)
  local copies, waits for them, and re-layouts  3.31 us (3%)
    pallas_call x1, Pallas kernels, per_device(): pl.pallas_call(kernel, out_shape=[jax.ShapeDtypeStruct((NTOK, 512), BF16)...  125 us
    unnamed x6, local copies, waits for them, and re-layouts  3.13 us

profile of v2, /device:TPU:0, one launch (start us, length us, event | category | flops | bytes accessed | tf_op | source)
XLA Modules:
  0.0 129.5 jit_solution(15484911019711507522)
XLA Ops:
  0.6 0.0 copy-start.1
  0.7 0.7 copy-done.1
  1.3 0.1 broadcast_add_fusion
  1.4 0.1 reshape.38
  1.5 0.1 eq.19
  1.6 0.7 fusion.marks_ref
  2.3 124.7 %shard_map.203 = (bf16[288,512]{1,0:T(8,128)(2,1)}, bf16[288,512]{1,0:T(8,128)(2,1)}) custom-call(bf16[288,512]{1,0:T(8,128)(2,1)} %bitcast.14, bf16[288,512]{1,0:T(8,128)(2,1)} %bitcast.15, bf16[2,144,128]{2,1,0:T(8,128)(2,1)} %fusion.marks_ref, f32[8]{0:T(128)} %temper_fine.1, f32[16]{0:T(128)} %temper_coarse.1, f32[1,512]{1,0:T(1,128)} %bitcast.19, ...), custom_call_target="tpu_custom_call" | custom-call | tf_op jit(solution)/shard_map/pallas_call | solution.py:588
  127.0 0.0 copy-start
  127.0 1.7 %copy.28 = bf16[2,6,24,512]{3,2,1,0:T(8,128)(2,1)} copy(bf16[2,6,24,512]{3,2,1,0:T(8,128)(2,1)} %bitcast.13) | data formatting | bytes 589824
  128.8 0.0 copy-done
  128.8 0.7 copy.29
  (2 shorter events, 0.0 us)
Async XLA Ops:
  0.6 0.7 copy-start.1
  127.0 1.8 %copy-start = (bf16[288,512]{1,0:T(8,128)(2,1)S(1)}, bf16[288,512]{1,0:T(8,128)(2,1)}, u32[]{:S(2)}) copy-start(bf16[288,512]{1,0:T(8,128)(2,1)} %get-tuple-element.5) | copy-start | bytes 884740

commit v3 on v2

--- a/solution.py
+++ b/solution.py
@@ -119,7 +119,7 @@
         mixed[rows, pl.ds(pl.multiple_of(p * 128, 128), 128)] = jnp.where(low, mixes[0], mixes[1]).astype(BF16)
         return carry
 
-    lax.fori_loop(start, stop, pair, 0)
+    lax.fori_loop(start, stop, pair, 0, unroll=2)
 
 
 def attend_backward(act, grad_mixed, grad_act, chances, rows, first, temper, temper_at, heads):
@@ -149,7 +149,7 @@
         grad_act[rows, at[2]] = gv.astype(BF16)
         return carry
 
-    lax.fori_loop(0, 4, pair, 0)
+    lax.fori_loop(0, 4, pair, 0, unroll=2)
 
 
 WEIGHTS = (
@@ -408,15 +408,15 @@
     gm = dot(to_merged[...], g_ref[...]).astype(BF16)
     allowed = [dot(marks_ref[w], marks_ref[w], TRANS_B) for w in range(2)]
     advance(*FINE)
-    advance("mwa", "mwb")
+    advance("mwa", "mwb", "co")
     halo_wait(0, buf0, behind)
     region = dot(region_table[...], buf0[...])
     unit, _ = normalise(region)
     region = (unit * gain_fine[...]).astype(BF16)
     advance(*FINE)
-    advance("mwa", "mwb")
+    advance("mwa", "mwb", "co")
     advance(*FINE)
-    advance("mwa", "mwb", "cq")
+    advance("mwa", "mwb", "co", "cq")
     finish("fq", "fk", "fv")
 
     def all_rows(ref, columns=slice(None)):
@@ -425,9 +425,9 @@
 
     for t, weight in enumerate((fq, fk, fv)):
         act[:, pl.ds(t * 512, 512)] = dot(region, all_rows(weight)).astype(BF16)
-    advance("mwa", "mwb")
+    advance("mwa", "mwb", "co")
     heads = (0, 128, 512)
-    then = (("mwa", "mwb", "co"), ("cq",), ("co",), ("cq", "spa", "spb"))
+    then = (("mwa", "mwb", "co", "spa", "spb"), ("cq", "spa", "spb"), ("spa", "spb"), ("cq", "spa", "spb"))
     for w in range(2):
         rows = pl.ds(w * NWIN, NWIN)
         for half in range(2):
@@ -437,11 +437,11 @@
     delta = dot(mixed[...], all_rows(fo)).astype(BF16)
     buf1[pl.ds(0, NTOK), :] = delta
     halo_send(1, halo_table, delta, buf1, sbuf1, ahead)
-    advance("mwa", "mwb", "co", "spa", "spb", "cq")
+    advance("mwa", "mwb", "spa", "spb", "cq")
     halo_wait(1, buf1, ahead)
     hidden = (xm_ref[...].astype(F32) + dot(back_table[...], buf1[...])).astype(BF16)
     hid[...] = hidden
-    advance("mwa", "mwb", "co", "spa", "spb")
+    advance("mwa", "mwb", "co")
 
     def cells(values):
         return jnp.concatenate([values[NMINE * i:NMINE * (i + 1)] for i in range(4)], axis=1)

time: 132 us -> 119 us (0.902)
  Pallas kernels: 125 us -> 112 us
    pallas_call x1, Pallas kernels: 125 us -> 112 us  [per_device(): pl.pallas_call(kernel, out_shape=[jax.ShapeDtypeStruct((NTOK, 512), BF16)...]
where the time goes in v3:
time: 119 us; the launch traced here: 117 us
  Pallas kernels  112 us (94%)
  local copies, waits for them, and re-layouts  3.31 us (3%)
    pallas_call x1, Pallas kernels, per_device(): pl.pallas_call(kernel, out_shape=[jax.ShapeDtypeStruct((NTOK, 512), BF16)...  112 us
    unnamed x6, local copies, waits for them, and re-layouts  3.13 us

profile of v3, /device:TPU:0, one launch (start us, length us, event | category | flops | bytes accessed | tf_op | source)
XLA Modules:
  0.0 116.9 jit_solution(3200246868541317394)
XLA Ops:
  0.6 0.0 copy-start.1
  0.7 0.7 copy-done.1
  1.3 0.1 broadcast_add_fusion
  1.4 0.1 reshape.38
  1.5 0.1 eq.19
  1.6 0.7 fusion.marks_ref
  2.3 112.1 %shard_map.203 = (bf16[288,512]{1,0:T(8,128)(2,1)}, bf16[288,512]{1,0:T(8,128)(2,1)}) custom-call(bf16[288,512]{1,0:T(8,128)(2,1)} %bitcast.14, bf16[288,512]{1,0:T(8,128)(2,1)} %bitcast.15, bf16[2,144,128]{2,1,0:T(8,128)(2,1)} %fusion.marks_ref, f32[8]{0:T(128)} %temper_fine.1, f32[16]{0:T(128)} %temper_coarse.1, f32[1,512]{1,0:T(1,128)} %bitcast.19, ...), custom_call_target="tpu_custom_call" | custom-call | tf_op jit(solution)/shard_map/pallas_call | solution.py:588
  114.5 0.0 copy-start
  114.5 1.7 %copy.28 = bf16[2,6,24,512]{3,2,1,0:T(8,128)(2,1)} copy(bf16[2,6,24,512]{3,2,1,0:T(8,128)(2,1)} %bitcast.13) | data formatting | bytes 589824
  116.2 0.0 copy-done
  116.2 0.7 copy.29
  (2 shorter events, 0.0 us)
Async XLA Ops:
  0.6 0.7 copy-start.1
  114.5 1.8 %copy-start = (bf16[288,512]{1,0:T(8,128)(2,1)S(1)}, bf16[288,512]{1,0:T(8,128)(2,1)}, u32[]{:S(2)}) copy-start(bf16[288,512]{1,0:T(8,128)(2,1)} %get-tuple-element.5) | copy-start | bytes 884740

commit v4 on v3

--- a/solution.py
+++ b/solution.py
@@ -149,7 +149,7 @@
         grad_act[rows, at[2]] = gv.astype(BF16)
         return carry
 
-    lax.fori_loop(0, 4, pair, 0, unroll=2)
+    lax.fori_loop(0, 4, pair, 0, unroll=4)
 
 
 WEIGHTS = (
@@ -486,7 +486,7 @@
         gnext_ref[:, pl.ds(pl.multiple_of(n * 256, 256), 256)] = total.astype(BF16).astype(F32)
         return carry
 
-    lax.fori_loop(0, 4, grad_step, 0)
+    lax.fori_loop(0, 4, grad_step, 0, unroll=True)
     grad_next = gnext_ref[...]
     pair_send(2, grad_next, psz, prz)
     coarse_next = (coarse + (partial + pair_wait(1, pry))).astype(BF16)

time: 119 us -> 117 us (0.983)
  no operation moved by 1% of the time
where the time goes in v4:
time: 117 us; the launch traced here: 116 us
  Pallas kernels  111 us (95%)
  local copies, waits for them, and re-layouts  3.31 us (3%)
    pallas_call x1, Pallas kernels, per_device(): pl.pallas_call(kernel, out_shape=[jax.ShapeDtypeStruct((NTOK, 512), BF16)...  111 us
    unnamed x6, local copies, waits for them, and re-layouts  3.13 us

profile of v4, /device:TPU:0, one launch (start us, length us, event | category | flops | bytes accessed | tf_op | source)
XLA Modules:
  0.0 115.8 jit_solution(5667223685488942573)
XLA Ops:
  0.6 0.0 copy-start.1
  0.7 0.7 copy-done.1
  1.3 0.1 broadcast_add_fusion
  1.4 0.1 reshape.38
  1.5 0.1 eq.19
  1.6 0.7 fusion.marks_ref
  2.3 111.0 %shard_map.203 = (bf16[288,512]{1,0:T(8,128)(2,1)}, bf16[288,512]{1,0:T(8,128)(2,1)}) custom-call(bf16[288,512]{1,0:T(8,128)(2,1)} %bitcast.14, bf16[288,512]{1,0:T(8,128)(2,1)} %bitcast.15, bf16[2,144,128]{2,1,0:T(8,128)(2,1)} %fusion.marks_ref, f32[8]{0:T(128)} %temper_fine.1, f32[16]{0:T(128)} %temper_coarse.1, f32[1,512]{1,0:T(1,128)} %bitcast.19, ...), custom_call_target="tpu_custom_call" | custom-call | tf_op jit(solution)/shard_map/pallas_call | solution.py:588
  113.4 0.0 copy-start
  113.4 1.7 %copy.28 = bf16[2,6,24,512]{3,2,1,0:T(8,128)(2,1)} copy(bf16[2,6,24,512]{3,2,1,0:T(8,128)(2,1)} %bitcast.13) | data formatting | bytes 589824
  115.1 0.0 copy-done
  115.1 0.7 copy.29
  (2 shorter events, 0.0 us)
Async XLA Ops:
  0.6 0.7 copy-start.1
  113.4 1.8 %copy-start = (bf16[288,512]{1,0:T(8,128)(2,1)S(1)}, bf16[288,512]{1,0:T(8,128)(2,1)}, u32[]{:S(2)}) copy-start(bf16[288,512]{1,0:T(8,128)(2,1)} %get-tuple-element.5) | copy-start | bytes 884740
